TPU v7x, 32 devices: a whole 2x2x4 slice. The times are simulated.
32 devices in a mesh: dp: 16 (over z, x, core), seq: 2 (over y).
Axes of the slice: x: 2, y: 2, z: 4, core: 2. Of those that a mesh axis runs over, the one named last changes fastest.
Arguments:
- hidden_in: bfloat16 [16, 1024, 1024], P('dp', 'seq'), may hold values from -6 to 6
- cond_in: bfloat16 [16, 1024], P('dp'), may hold values from -6 to 6
- ada_weight: bfloat16 [1024, 6144], P(('dp', 'seq')), may hold values from -0.1875 to 0.1875
- ada_bias: bfloat16 [6144], P(('dp', 'seq')), may hold values from -3 to 3
- qkv_weight: bfloat16 [1024, 3072], P(('dp', 'seq')), may hold values from -0.1875 to 0.1875
- qv_bias: bfloat16 [2048], P(('dp', 'seq')), may hold values from -3 to 3
- proj_weight: bfloat16 [1024, 1024], P(('dp', 'seq')), may hold values from -1 to 1
- proj_bias: bfloat16 [1024], P(('dp', 'seq')), may hold values from -3 to 3
- up_weight: bfloat16 [1024, 4096], P(('dp', 'seq')), may hold values from -0.1875 to 0.1875
- up_bias: bfloat16 [4096], P(('dp', 'seq')), may hold values from -3 to 3
- down_weight: bfloat16 [4096, 1024], P(('dp', 'seq')), may hold values from -0.09375 to 0.09375
- down_bias: bfloat16 [1024], P(('dp', 'seq')), may hold values from -3 to 3
- out_cot: bfloat16 [16, 1024, 1024], P('dp', 'seq'), may hold values from -6 to 6
Outputs:
- mixed_out: bfloat16 [16, 1024, 1024], P('dp', 'seq')
- grad_input: float32 [16, 1024, 1024], P('dp', 'seq')
- grad_cond: float32 [16, 1024], P('dp')
- grad_ada_weight: float32 [1024, 6144], P(('dp', 'seq'))
- grad_ada_bias: float32 [6144], P(('dp', 'seq'))
- grad_qkv_weight: float32 [1024, 3072], P(('dp', 'seq'))
- grad_qv_bias: float32 [2048], P(('dp', 'seq'))
- grad_proj_weight: float32 [1024, 1024], P(('dp', 'seq'))
- grad_proj_bias: float32 [1024], P(('dp', 'seq'))
- grad_up_weight: float32 [1024, 4096], P(('dp', 'seq'))
- grad_up_bias: float32 [4096], P(('dp', 'seq'))
- grad_down_weight: float32 [4096, 1024], P(('dp', 'seq'))
- grad_down_bias: float32 [1024], P(('dp', 'seq'))
All inputs are finite; a program needn't handle non-finite values.
Results may differ from a plain program's by a relative error of at most 0.012.
The roundings to bfloat16 on the way count: a program that leaves them out, or rounds other values in their place, can miss the bound.
Values may be sent and summed in bfloat16 or wider, within the bound.
A program may use at most 256 MiB of HBM per device.

v0:
```python
import math

import jax
import jax.numpy as jnp
from jax import lax
from jax.sharding import PartitionSpec as P

H = 16


norm_eps = 1e-06
exact_mode = lax.Precision.HIGHEST


def normalize_rows(values):
    centre = values - jnp.mean(values, axis=-1, keepdims=True)
    inv_std = lax.rsqrt(jnp.mean(centre * centre, axis=-1, keepdims=True) + norm_eps)
    return (centre * inv_std, inv_std)


def norm_back(grad_norm, normed, inv_std):
    first_mean = jnp.mean(grad_norm, axis=-1, keepdims=True)
    second_mean = jnp.mean(grad_norm * normed, axis=-1, keepdims=True)
    return inv_std * (grad_norm - first_mean - normed * second_mean)


def gelu_tanh(inputs):
    return jax.nn.gelu(inputs, approximate=True)


def halves(matrix):
    middle_col = matrix.shape[1] // 2
    return (matrix[:, :middle_col], matrix[:, middle_col:])


def attend_block(item):
    queries, keys_one, values_one = item
    root = math.sqrt(queries.shape[-1])
    scores = (
        jnp.einsum("qhd,khd->hqk", queries, keys_one, preferred_element_type=jnp.float32) / root
    )
    peak = jnp.max(scores, axis=-1, keepdims=True)
    expo = jnp.exp(scores - peak)
    total = jnp.sum(expo, axis=-1, keepdims=True)
    probs_low = (expo / total).astype(jnp.bfloat16)
    output = jnp.einsum("hqk,khd->qhd", probs_low, values_one, preferred_element_type=jnp.float32)
    return (output.astype(jnp.bfloat16), (peak + jnp.log(total))[..., 0])


def attend_back(item):
    queries, keys_one, values_one, grad_output, logsum = item
    root = math.sqrt(queries.shape[-1])
    scores = (
        jnp.einsum("qhd,khd->hqk", queries, keys_one, preferred_element_type=jnp.float32) / root
    )
    probs = jnp.exp(scores - logsum[..., None])
    grad_probs = jnp.einsum(
        "qhd,khd->hqk", grad_output, values_one, preferred_element_type=jnp.float32
    )
    inner = jnp.sum(probs * grad_probs, axis=-1, keepdims=True)
    grad_scores = (probs * (grad_probs - inner)).astype(jnp.bfloat16)
    grad_values = jnp.einsum(
        "hqk,qhd->khd", probs.astype(jnp.bfloat16), grad_output, preferred_element_type=jnp.float32
    )
    grad_queries = (
        jnp.einsum("hqk,khd->qhd", grad_scores, keys_one, preferred_element_type=jnp.float32) / root
    )
    grad_keys = (
        jnp.einsum("hqk,qhd->khd", grad_scores, queries, preferred_element_type=jnp.float32) / root
    )
    length = queries.shape[0]
    stacked = jnp.stack([grad_queries, grad_keys, grad_values], axis=1)
    return stacked.reshape(length, 3, -1).astype(jnp.bfloat16)


def per_device(
    hidden_in,
    cond_in,
    ada_weight,
    ada_bias,
    qkv_weight,
    qv_bias,
    proj_weight,
    proj_bias,
    up_weight,
    up_bias,
    down_weight,
    down_bias,
    out_cot,
):
    params = (
        ada_weight,
        ada_bias,
        qkv_weight,
        qv_bias,
        proj_weight,
        proj_bias,
        up_weight,
        up_bias,
        down_weight,
        down_bias,
    )
    gathered = (
        lax.all_gather(params[0], ("dp", "seq"), axis=0, tiled=True),
        lax.all_gather(params[1], ("dp", "seq"), axis=0, tiled=True),
        lax.all_gather(params[2], ("dp", "seq"), axis=0, tiled=True),
        lax.all_gather(params[3], ("dp", "seq"), axis=0, tiled=True),
        lax.all_gather(params[4], ("dp", "seq"), axis=0, tiled=True),
        lax.all_gather(params[5], ("dp", "seq"), axis=0, tiled=True),
        lax.all_gather(params[6], ("dp", "seq"), axis=0, tiled=True),
        lax.all_gather(params[7], ("dp", "seq"), axis=0, tiled=True),
        lax.all_gather(params[8], ("dp", "seq"), axis=0, tiled=True),
        lax.all_gather(params[9], ("dp", "seq"), axis=0, tiled=True),
    )
    ada_full = gathered[0]
    qkv_full = gathered[2]
    proj_full = gathered[4]
    up_full = gathered[6]
    down_full = gathered[8]
    groups, local_len, model_width = hidden_in.shape
    row_count = groups * local_len
    cond_float = cond_in.astype(jnp.float32)
    cond_act = jax.nn.silu(cond_float).astype(jnp.bfloat16)
    modul = jnp.dot(cond_act, ada_full, preferred_element_type=jnp.float32) + gathered[1].astype(
        jnp.float32
    )
    modul = modul.reshape(groups, 6, 1, model_width)
    shift_att = modul[:, 0]
    scale_att = modul[:, 1]
    gate_att = modul[:, 2]
    shift_mlp = modul[:, 3]
    scale_mlp = modul[:, 4]
    gate_mlp = modul[:, 5]
    source = hidden_in.astype(jnp.float32)
    normed_one, inv_one = normalize_rows(source)
    first_in = (normed_one * (1.0 + scale_att) + shift_att).astype(jnp.bfloat16)
    first_flat = first_in.reshape(row_count, model_width)
    qv_full = gathered[3].astype(jnp.float32)
    zero_bias = jnp.zeros((model_width,), jnp.float32)
    qkv_bias = jnp.concatenate([qv_full[:model_width], zero_bias, qv_full[model_width:]])
    mixed = jnp.dot(first_flat, qkv_full, preferred_element_type=jnp.float32) + qkv_bias
    mixed = mixed.astype(jnp.bfloat16).reshape(groups, local_len, 3, model_width)
    heads = lax.all_to_all(mixed, "seq", split_axis=3, concat_axis=1, tiled=True)
    seq_len = heads.shape[1]
    group_w = heads.shape[3]
    head_dim = model_width // H
    heads_here = group_w // head_dim
    queries = heads[:, :, 0].reshape(groups, seq_len, heads_here, head_dim)
    keys_all = heads[:, :, 1].reshape(groups, seq_len, heads_here, head_dim)
    values_all = heads[:, :, 2].reshape(groups, seq_len, heads_here, head_dim)
    attended, logsum = lax.map(attend_block, (queries, keys_all, values_all))
    attended = attended.reshape(groups, seq_len, group_w)
    back_tokens = lax.all_to_all(attended, "seq", split_axis=1, concat_axis=2, tiled=True)
    attended_flat = back_tokens.reshape(row_count, model_width)
    branch = jnp.dot(attended_flat, proj_full, preferred_element_type=jnp.float32) + gathered[
        5
    ].astype(jnp.float32)
    branch = branch.reshape(groups, local_len, model_width)
    middle = source + gate_att * branch
    normed_two, inv_two = normalize_rows(middle)
    second_in = (normed_two * (1.0 + scale_mlp) + shift_mlp).astype(jnp.bfloat16)
    second_flat = second_in.reshape(row_count, model_width)
    up_pre = jnp.dot(second_flat, up_full, preferred_element_type=jnp.float32) + gathered[7].astype(
        jnp.float32
    )
    act_value, gelu_pull = jax.vjp(gelu_tanh, up_pre)
    act_low = act_value.astype(jnp.bfloat16)
    mlp_out = jnp.dot(act_low, down_full, preferred_element_type=jnp.float32) + gathered[9].astype(
        jnp.float32
    )
    mlp_out = mlp_out.reshape(groups, local_len, model_width)
    result = (middle + gate_mlp * mlp_out).astype(jnp.bfloat16)
    again = (
        lax.all_gather(params[0], ("dp", "seq"), axis=0, tiled=True),
        lax.all_gather(params[1], ("dp", "seq"), axis=0, tiled=True),
        lax.all_gather(params[2], ("dp", "seq"), axis=0, tiled=True),
        lax.all_gather(params[3], ("dp", "seq"), axis=0, tiled=True),
        lax.all_gather(params[4], ("dp", "seq"), axis=0, tiled=True),
        lax.all_gather(params[5], ("dp", "seq"), axis=0, tiled=True),
        lax.all_gather(params[6], ("dp", "seq"), axis=0, tiled=True),
        lax.all_gather(params[7], ("dp", "seq"), axis=0, tiled=True),
        lax.all_gather(params[8], ("dp", "seq"), axis=0, tiled=True),
        lax.all_gather(params[9], ("dp", "seq"), axis=0, tiled=True),
    )
    ada_back = again[0]
    qkv_back_w = again[2]
    proj_back = again[4]
    up_back = again[6]
    down_back = again[8]
    grad_out = out_cot.astype(jnp.float32)
    grad_gate_mlp = jnp.sum(grad_out * mlp_out, axis=1)
    grad_mlp = (grad_out * gate_mlp).astype(jnp.bfloat16).reshape(row_count, model_width)
    grad_down_w = jnp.dot(act_low.T, grad_mlp, preferred_element_type=jnp.float32)
    grad_down_b = jnp.sum(grad_mlp.astype(jnp.float32), axis=0)
    grad_act = jnp.dot(grad_mlp, down_back.T, preferred_element_type=jnp.float32)
    grad_up = gelu_pull(grad_act)[0].astype(jnp.bfloat16)
    grad_up_w = jnp.dot(second_flat.T, grad_up, preferred_element_type=jnp.float32)
    grad_up_b = jnp.sum(grad_up.astype(jnp.float32), axis=0)
    grad_second = jnp.dot(grad_up, up_back.T, preferred_element_type=jnp.float32).reshape(
        groups, local_len, model_width
    )
    grad_shift_mlp = jnp.sum(grad_second, axis=1)
    grad_scale_mlp = jnp.sum(grad_second * normed_two, axis=1)
    grad_middle = grad_out + norm_back(grad_second * (1.0 + scale_mlp), normed_two, inv_two)
    grad_gate_att = jnp.sum(grad_middle * branch, axis=1)
    grad_branch = (grad_middle * gate_att).astype(jnp.bfloat16).reshape(row_count, model_width)
    grad_proj_w = jnp.dot(attended_flat.T, grad_branch, preferred_element_type=jnp.float32)
    grad_proj_b = jnp.sum(grad_branch.astype(jnp.float32), axis=0)
    grad_attended = jnp.dot(grad_branch, proj_back.T, preferred_element_type=jnp.float32)
    grad_attended = grad_attended.astype(jnp.bfloat16).reshape(groups, local_len, model_width)
    grad_heads = lax.all_to_all(grad_attended, "seq", split_axis=2, concat_axis=1, tiled=True)
    grad_heads = grad_heads.reshape(groups, seq_len, heads_here, head_dim)
    grad_mixed = lax.map(attend_back, (queries, keys_all, values_all, grad_heads, logsum))
    grad_local = lax.all_to_all(grad_mixed, "seq", split_axis=1, concat_axis=3, tiled=True)
    grad_flat = grad_local.reshape(row_count, 3 * model_width)
    grad_qkv_w = jnp.dot(first_flat.T, grad_flat, preferred_element_type=jnp.float32)
    bias_total = jnp.sum(grad_flat.astype(jnp.float32), axis=0)
    grad_qv_b = jnp.concatenate([bias_total[:model_width], bias_total[2 * model_width :]])
    grad_first = jnp.dot(grad_flat, qkv_back_w.T, preferred_element_type=jnp.float32).reshape(
        groups, local_len, model_width
    )
    grad_shift_att = jnp.sum(grad_first, axis=1)
    grad_scale_att = jnp.sum(grad_first * normed_one, axis=1)
    grad_input = grad_middle + norm_back(grad_first * (1.0 + scale_att), normed_one, inv_one)
    grad_modul = jnp.stack(
        [
            grad_shift_att,
            grad_scale_att,
            grad_gate_att,
            grad_shift_mlp,
            grad_scale_mlp,
            grad_gate_mlp,
        ],
        axis=1,
    )
    grad_modul = grad_modul.reshape(groups, 6 * model_width)
    silu_value, silu_pull = jax.vjp(jax.nn.silu, cond_float)
    cond_wide = cond_act.astype(jnp.float32)
    up_left, up_right = halves(grad_up_w)
    down_left, down_right = halves(grad_down_w)
    grad_ada_w = jnp.dot(cond_wide.T, grad_modul, precision=exact_mode)
    grad_ada_b = jnp.sum(grad_modul, axis=0)
    ada_left, ada_right = halves(grad_ada_w)
    cond_part = jnp.dot(grad_modul, ada_back.astype(jnp.float32).T, precision=exact_mode)
    cond_total = lax.psum(cond_part, "seq")
    grad_condition = silu_pull(cond_total)[0]
    owned = (
        lax.psum_scatter(ada_left, ("dp", "seq"), scatter_dimension=0, tiled=True),
        lax.psum_scatter(ada_right, ("dp", "seq"), scatter_dimension=0, tiled=True),
        lax.psum_scatter(grad_ada_b, ("dp", "seq"), scatter_dimension=0, tiled=True),
        lax.psum_scatter(grad_qkv_w, ("dp", "seq"), scatter_dimension=0, tiled=True),
        lax.psum_scatter(grad_qv_b, ("dp", "seq"), scatter_dimension=0, tiled=True),
        lax.psum_scatter(grad_proj_w, ("dp", "seq"), scatter_dimension=0, tiled=True),
        lax.psum_scatter(grad_proj_b, ("dp", "seq"), scatter_dimension=0, tiled=True),
        lax.psum_scatter(up_left, ("dp", "seq"), scatter_dimension=0, tiled=True),
        lax.psum_scatter(up_right, ("dp", "seq"), scatter_dimension=0, tiled=True),
        lax.psum_scatter(grad_up_b, ("dp", "seq"), scatter_dimension=0, tiled=True),
        lax.psum_scatter(down_left, ("dp", "seq"), scatter_dimension=0, tiled=True),
        lax.psum_scatter(down_right, ("dp", "seq"), scatter_dimension=0, tiled=True),
        lax.psum_scatter(grad_down_b, ("dp", "seq"), scatter_dimension=0, tiled=True),
    )
    own_ada_w = jnp.concatenate([owned[0], owned[1]], axis=1)
    own_ada_b = owned[2]
    others = owned[3:]
    own_up_w = jnp.concatenate([others[4], others[5]], axis=1)
    own_down_w = jnp.concatenate([others[7], others[8]], axis=1)
    return (
        result,
        grad_input,
        grad_condition,
        own_ada_w,
        own_ada_b,
        others[0],
        others[1],
        others[2],
        others[3],
        own_up_w,
        others[6],
        own_down_w,
        others[9],
    )


def solution(mesh):
    placed = (
        P("dp", "seq", None),
        P("dp", None),
        P(("dp", "seq"), None),
        P(("dp", "seq")),
        P(("dp", "seq"), None),
        P(("dp", "seq")),
        P(("dp", "seq"), None),
        P(("dp", "seq")),
        P(("dp", "seq"), None),
        P(("dp", "seq")),
        P(("dp", "seq"), None),
        P(("dp", "seq")),
        P("dp", "seq", None),
    )
    return jax.shard_map(
        per_device,
        mesh=mesh,
        in_specs=placed,
        out_specs=(
            P("dp", "seq", None),
            P("dp", "seq", None),
            P("dp", None),
            P(("dp", "seq"), None),
            P(("dp", "seq")),
            P(("dp", "seq"), None),
            P(("dp", "seq")),
            P(("dp", "seq"), None),
            P(("dp", "seq")),
            P(("dp", "seq"), None),
            P(("dp", "seq")),
            P(("dp", "seq"), None),
            P(("dp", "seq")),
        ),
        check_vma=False,
    )
```

profile of v0, /device:TPU:0, one launch (start us, length us, event | category | flops | bytes accessed | tf_op | source)
XLA Modules:
  0.0 1855.5 jit_solution(7762786034650628124)
XLA Ops:
  18.3 43.4 %all-reduce.10 = (bf16[2048]{0:T(1024)(128)(2,1)S(1)}, bf16[6144]{0:T(1024)(128)(2,1)S(1)}, bf16[1024]{0:T(1024)(128)(2,1)S(1)}, bf16[1024]{0:T(1024)(128)(2,1)}) all-reduce(bf16[2048]{0:T(1024)(128)(2,1)S(1)} %dynamic-update-slice.1, bf16[6144]{0:T(1024)(128)(2,1)S(1)} %dynamic-update-slice, ...), channel_id=1, replica_groups=mesh['dp'=16,'seq'=2] {'dp','seq'}, use_global_device_ids=true, to_apply=%add.1 | all-reduce | flops 10240 | bytes 40960
  61.7 48.4 %all-gather.7.cloned.1.call-done = bf16[1024,6144]{1,0:T(8,128)(2,1)} async-done(((bf16[32,6144]{1,0:T(8,128)(2,1)}), bf16[1024,6144]{1,0:T(8,128)(2,1)}) %all-gather.7.cloned.1.call-update) | async-done | bytes 12582928 | tf_op jit(solution)/shard_map/all_gather | solution.py:104
  110.1 6.4 fusion.50
  116.6 64.2 %all-gather.9.cloned.1.call-done = bf16[1024,3072]{1,0:T(8,128)(2,1)} async-done(((bf16[32,3072]{1,0:T(8,128)(2,1)}), bf16[1024,3072]{1,0:T(8,128)(2,1)}) %all-gather.9.cloned.1.call-update) | async-done | bytes 6291472 | tf_op jit(solution)/shard_map/all_gather | solution.py:106
  180.8 7.8 add_convert_fusion
  188.7 3.2 copy.74
  191.9 2.7 copy.75
  194.6 55.5 %all_to_all.63 = bf16[1,512,3,1024]{1,2,0,3:T(4,128)(2,1)S(1)} all-to-all(bf16[1,512,3,1024]{1,2,0,3:T(4,128)(2,1)S(1)} %copy.75), channel_id=1, replica_groups=mesh['dp'=16,'seq'=2] {'seq'}, dimensions={3} | all-to-all | bytes 6291456 | tf_op jit(solution)/shard_map/all_to_all | solution.py:143
  250.9 2.9 copy.77
  253.8 3.1 fusion.70
  257.9 1.9 copy.78
  259.8 13.4 multiply_reduce_fusion.1
  273.2 13.6 fusion
  286.8 15.2 fusion.36
  302.0 4.8 copy.82
  307.4 7.0 reduce.21
  316.1 4.4 all-to-all-start.1
  320.6 70.7 %all-gather = bf16[32,1,128]{2,1,0:T(2,128)(2,1)S(1)} all-gather(bf16[1,1,128]{2,1,0:T(2,128)(2,1)S(1)} %bitcast.212), channel_id=1, replica_groups=mesh['dp'=16,'seq'=2] {'dp','seq'}, dimensions={0}, use_global_device_ids=true | all-gather | bytes 8448 | tf_op jit(solution)/shard_map/all_gather | solution.py:111
  391.3 2.2 reshape.341
  394.8 2.3 copy.83
  397.1 4.7 fusion.66
  402.3 10.4 fusion.60
  412.7 9.0 fusion.42
  421.7 6.7 fusion.68
  429.3 16.7 convert_reduce_fusion
  446.0 6.8 fusion.58
  452.8 6.4 fusion.69
  459.9 8.4 fusion.63
  468.3 11.9 fusion.27
  480.2 2.4 convert_reduce_fusion.4
  486.8 7.0 reduce.22
  495.4 3.6 all-to-all-start.2
  499.8 23.6 %all-to-all-done.2 = bf16[2,2,131072]{2,1,0:T(2,128)(2,1)S(1)} async-done(((bf16[2,2,131072]{2,1,0:T(2,128)(2,1)}), bf16[2,2,131072]{2,1,0:T(2,128)(2,1)S(1)}, u32[]{:S(2)}, u32[]{:S(2)}) %all-to-all-start.2) | async-done | bytes 1048608 | tf_op jit(solution)/shard_map/all_to_all | solution.py:211
  526.8 14.0 fusion.33
  540.8 3.9 copy.91
  544.7 22.5 %multiply_reduce_fusion = (f32[8,1024]{1,0:T(8,128)S(1)}, f32[8,1024,1024]{1,2,0:T(8,128)}) fusion(f32[8,1024,1024]{1,2,0:T(8,128)} %get-tuple-element.103, f32[8,1024]{1,0:T(8,128)S(1)} %log_add_fusion, bf16[1024,8,64]{0,2,1:T(8,128)(2,1)S(1)} %squeeze.37, bf16[1024,8,64]{0,2,1:T(8,128)(2,1)S(1)} %bitcast.166), kind=kOutput, calls=%fused_computation.1 | convolution fusion | flops 1107288064 | bytes 69271552 | tf_op jit(solution)/shard_map/while/body/eval_jaxpr/qhd,khd->hqk/dot_general | solution.py:57
  567.3 28.7 %multiply_convert_fusion = bf16[8,1024,1024]{1,2,0:T(8,128)(2,1)} fusion(f32[8,1024,1024]{1,2,0:T(8,128)} %get-tuple-element.107, f32[8,1024,1024]{1,2,0:T(8,128)} %get-tuple-element.103, f32[8,1024]{1,0:T(8,128)S(1)} %get-tuple-element.106, f32[8,1024]{1,0:T(8,128)S(1)} %log_add_fusion), kind=kLoop, calls=%fused_computation | loop fusion | flops 41943040 | bytes 83951616 | tf_op jit(solution)/shard_map/while/body/eval_jaxpr/convert_element_type | solution.py:61
  596.0 11.1 multiply_convert_fusion.2
  607.1 4.1 copy.90
  611.2 8.9 multiply_convert_fusion.3
  620.1 3.9 copy.89
  624.0 9.4 pad_maximum_fusion
  633.5 5.7 all-to-all-start.3
  639.3 91.6 %all-to-all-done.3 = bf16[1,1024,3,512]{3,2,0,1:T(4,128)(2,1)} async-done(((bf16[1,1024,3,512]{3,2,0,1:T(4,128)(2,1)}), bf16[1,1024,3,512]{3,2,0,1:T(4,128)(2,1)}, u32[]{:S(2)}, u32[]{:S(2)}) %all-to-all-start.3) | async-done | bytes 3145760 | tf_op jit(solution)/shard_map/all_to_all | solution.py:214
  730.9 3.0 copy.92
  734.0 2.8 copy.93
  736.8 8.2 fusion.24
  745.4 2.3 fusion.29
  747.7 11.7 broadcast_multiply_fusion
  759.4 19.5 %fusion.67 = (f32[1024,3072]{1,0:T(8,128)}, f32[1024,3072]{1,0:T(8,128)}) fusion(f32[1024,6144]{1,0:T(8,128)} %broadcast_multiply_fusion), kind=kLoop, calls=%fused_computation.114 | loop fusion | bytes 50331648 | tf_op jit(solution)/shard_map/slice | solution.py:33
  779.7 4.8 fusion.74
  785.2 10.6 fusion.55
  796.5 39.9 %all-reduce.9 = (f32[6144]{0:T(1024)S(1)}, f32[2048]{0:T(1024)S(1)}, f32[1024]{0:T(1024)S(1)}, f32[4096]{0:T(1024)S(1)}, f32[1024]{0:T(1024)S(1)}) all-reduce(f32[6144]{0:T(1024)S(1)} %reshape.321, f32[2048]{0:T(1024)S(1)} %pad_maximum_fusion.5, ...), channel_id=4, replica_groups=mesh['dp'=16,'seq'=2] {'dp','seq'}, use_global_device_ids=true, to_apply=%region_20.21.clone | all-reduce | flops 14336 | bytes 114688
  839.4 12.8 fusion.73
  852.2 5.5 psum.7
  858.3 1.9 pad_maximum_fusion.3
  860.1 177.3 %reduce-scatter.17.cloned.1.call-done = f32[32,2048]{1,0:T(8,128)} async-done(((f32[1024,2048]{1,0:T(8,128)}), f32[32,2048]{1,0:T(8,128)}) %reduce-scatter.17.cloned.1.call-update) | async-done | bytes 262160 | tf_op jit(solution)/shard_map/reduce_scatter | solution.py:255
  1037.4 185.8 %reduce-scatter.19.cloned.1.call-done = f32[32,2048]{1,0:T(8,128)} async-done(((f32[1024,2048]{1,0:T(8,128)}), f32[32,2048]{1,0:T(8,128)}) %reduce-scatter.19.cloned.1.call-update) | async-done | bytes 262160 | tf_op jit(solution)/shard_map/reduce_scatter | solution.py:256
  1223.2 1.9 pad_maximum_fusion.2
  1225.1 159.8 %reduce-scatter.9.cloned.1.call-done = f32[32,3072]{1,0:T(8,128)} async-done(((f32[1024,3072]{1,0:T(8,128)}), f32[32,3072]{1,0:T(8,128)}) %reduce-scatter.9.cloned.1.call-update) | async-done | bytes 393232 | tf_op jit(solution)/shard_map/reduce_scatter | solution.py:248
  1384.9 161.6 %reduce-scatter.11.cloned.1.call-done = f32[32,3072]{1,0:T(8,128)} async-done(((f32[1024,3072]{1,0:T(8,128)}), f32[32,3072]{1,0:T(8,128)}) %reduce-scatter.11.cloned.1.call-update) | async-done | bytes 393232 | tf_op jit(solution)/shard_map/reduce_scatter | solution.py:249
  1546.5 2.0 pad_maximum_fusion.1
  1548.6 141.2 %reduce-scatter.15.cloned.1.call-done = f32[32,1024]{1,0:T(8,128)} async-done(((f32[1024,1024]{1,0:T(8,128)}), f32[32,1024]{1,0:T(8,128)}) %reduce-scatter.15.cloned.1.call-update) | async-done | bytes 131088 | tf_op jit(solution)/shard_map/reduce_scatter | solution.py:253
  1689.8 159.0 %reduce-scatter.13.cloned.1.call-done = f32[32,3072]{1,0:T(8,128)} async-done(((f32[1024,3072]{1,0:T(8,128)}), f32[32,3072]{1,0:T(8,128)}) %reduce-scatter.13.cloned.1.call-update) | async-done | bytes 393232 | tf_op jit(solution)/shard_map/reduce_scatter | solution.py:251
  (153 shorter events, 34.3 us)
Async XLA Ops:
  7.2 103.0 %all-gather.7.cloned.1.call-start = ((), (), s32[]{:S(2)}) async-start(), calls=%async_computation.12 | async-start | bytes 12976128 | tf_op jit(solution)/shard_map/all_gather | solution.py:104
  7.9 172.9 %all-gather.9.cloned.1.call-start = ((), (), s32[]{:S(2)}) async-start(), calls=%async_computation.13 | async-start | bytes 6488064 | tf_op jit(solution)/shard_map/all_gather | solution.py:106
  8.7 388.5 %all-gather.11.cloned.1.call-start = ((), (), s32[]{:S(2)}) async-start(), calls=%async_computation.14 | async-start | bytes 2162688 | tf_op jit(solution)/shard_map/all_gather | solution.py:108
  9.4 392.9 %all-gather.13.cloned.1.call-start = ((), (), s32[]{:S(2)}) async-start(), calls=%async_computation.15 | async-start | bytes 8650752 | tf_op jit(solution)/shard_map/all_gather | solution.py:110
  10.0 419.3 %all-gather.15.cloned.1.call-start = ((), (), s32[]{:S(2)}) async-start(), calls=%async_computation.16 | async-start | bytes 8650752 | tf_op jit(solution)/shard_map/all_gather | solution.py:112
  12.0 168.8 %copy-start.19 = (f32[512]{0:T(512)}, f32[512]{0:T(512)S(1)}, u32[]{:S(2)}) copy-start(f32[512]{0:T(512)S(1)} %broadcast_multiply_fusion.6) | copy-start | bytes 6148
  13.7 167.1 %copy-start.24 = (f32[512]{0:T(512)}, f32[512]{0:T(512)S(1)}, u32[]{:S(2)}) copy-start(f32[512]{0:T(512)S(1)} %add_rsqrt_fusion.1) | copy-start | bytes 6148
  15.0 101.6 %copy-start.15 = (f32[1,1024]{1,0:T(1,128)}, f32[1,1024]{1,0:T(1,128)S(1)}, u32[]{:S(2)}) copy-start(f32[1,1024]{1,0:T(1,128)S(1)} %get-tuple-element.73) | copy-start | bytes 12292
  110.1 70.7 %copy-start.4 = (bf16[1,512,1024]{2,1,0:T(8,128)(2,1)S(1)}, bf16[1,512,1024]{2,1,0:T(8,128)(2,1)}, u32[]{:S(2)}) copy-start(bf16[1,512,1024]{2,1,0:T(8,128)(2,1)} %param.13) | copy-start | bytes 3145732
  116.6 64.2 %copy-start.17 = (f32[1,1,1,1024]{3,2,1,0:T(1,128)}, f32[1,1,1,1024]{3,2,1,0:T(1,128)S(1)}, u32[]{:S(2)}) copy-start(f32[1,1,1,1024]{3,2,1,0:T(1,128)S(1)} %get-tuple-element.96) | copy-start | bytes 12292
  116.6 64.2 %copy-start.27 = (f32[1,1,1,1024]{3,2,1,0:T(1,128)}, f32[1,1,1,1024]{3,2,1,0:T(1,128)S(1)}, u32[]{:S(2)}) copy-start(f32[1,1,1,1024]{3,2,1,0:T(1,128)S(1)} %get-tuple-element.95) | copy-start | bytes 12292
  257.4 15.8 copy-start
  257.9 15.3 copy-start.2
  259.8 27.0 %copy-start.9 = (bf16[1,1024,1,512]{1,3,2,0:T(8,128)(2,1)}, bf16[1,1024,1,512]{1,3,2,0:T(8,128)(2,1)S(1)}, u32[]{:S(2)}) copy-start(bf16[1,1024,1,512]{1,3,2,0:T(8,128)(2,1)S(1)} %copy.78) | copy-start | bytes 3145732
  306.9 13.7 copy-start.30
  316.1 75.3 %all-to-all-start.1 = ((bf16[2,2,131072]{2,1,0:T(2,128)(2,1)}), bf16[2,2,131072]{2,1,0:T(2,128)(2,1)}, u32[]{:S(2)}, u32[]{:S(2)}) async-start(bf16[2,2,131072]{2,1,0:T(2,128)(2,1)} %reshape.340), calls=%async_computation.1 | async-start | bytes 2097152 | tf_op jit(solution)/shard_map/all_to_all | solution.py:153
  320.5 537.8 %reduce-scatter.21.cloned.1.call-start = ((), (), s32[]{:S(2)}) async-start(), calls=%async_computation.23 | async-start | bytes 8650752 | tf_op jit(solution)/shard_map/reduce_scatter | solution.py:258
  320.5 76.6 %copy-start.21 = (f32[1024]{0:T(1024)}, f32[1024]{0:T(1024)S(1)}, u32[]{:S(2)}) copy-start(f32[1024]{0:T(1024)S(1)} %convert_element_type.107) | copy-start | bytes 12292
  391.3 5.8 copy-start.5
  402.3 10.4 copy-start.12
  428.4 429.8 %reduce-scatter.23.cloned.1.call-start = ((), (), s32[]{:S(2)}) async-start(), calls=%async_computation.24 | async-start | bytes 8650752 | tf_op jit(solution)/shard_map/reduce_scatter | solution.py:259
  429.2 608.2 %reduce-scatter.17.cloned.1.call-start = ((), (), s32[]{:S(2)}) async-start(), calls=%async_computation.21 | async-start | bytes 8650752 | tf_op jit(solution)/shard_map/reduce_scatter | solution.py:255
  459.2 0.7 copy-start.29
  480.2 3.4 copy-start.31
  482.7 1.0 copy-start.13
  495.4 27.9 %all-to-all-start.2 = ((bf16[2,2,131072]{2,1,0:T(2,128)(2,1)}), bf16[2,2,131072]{2,1,0:T(2,128)(2,1)S(1)}, u32[]{:S(2)}, u32[]{:S(2)}) async-start(bf16[2,2,131072]{2,1,0:T(2,128)(2,1)} %reshape.342), calls=%async_computation.2 | async-start | bytes 2097152 | tf_op jit(solution)/shard_map/all_to_all | solution.py:211
  499.0 724.2 %reduce-scatter.19.cloned.1.call-start = ((), (), s32[]{:S(2)}) async-start(), calls=%async_computation.22 | async-start | bytes 8650752 | tf_op jit(solution)/shard_map/reduce_scatter | solution.py:256
  526.8 17.9 copy-start.10
  567.3 28.7 %copy-start.3 = (bf16[1,1024,1,512]{1,3,2,0:T(8,128)(2,1)S(1)}, bf16[1,1024,1,512]{1,3,2,0:T(8,128)(2,1)}, u32[]{:S(2)}) copy-start(bf16[1,1024,1,512]{1,3,2,0:T(8,128)(2,1)} %copy-done.2) | copy-start | bytes 3145732
  596.0 15.2 copy-start.1
  620.1 3.9 copy-start.7
  633.5 5.8 copy-start.26
  633.5 97.5 %all-to-all-start.3 = ((bf16[1,1024,3,512]{3,2,0,1:T(4,128)(2,1)}), bf16[1,1024,3,512]{3,2,0,1:T(4,128)(2,1)}, u32[]{:S(2)}, u32[]{:S(2)}) async-start(bf16[1,1024,3,512]{3,2,0,1:T(4,128)(2,1)} %pad_maximum_fusion), calls=%async_computation.3 | async-start | bytes 8388608 | tf_op jit(solution)/shard_map/all_to_all | solution.py:214
  639.2 745.7 %reduce-scatter.9.cloned.1.call-start = ((), (), s32[]{:S(2)}) async-start(), calls=%async_computation.17 | async-start | bytes 12976128 | tf_op jit(solution)/shard_map/reduce_scatter | solution.py:248
  733.9 2.9 copy-start.18
  733.9 2.9 copy-start.20
  733.9 2.8 copy-start.25
  736.8 8.6 copy-start.6
  736.8 8.6 copy-start.8
  736.8 8.6 copy-start.11
  736.8 8.6 copy-start.22
  778.9 767.6 %reduce-scatter.11.cloned.1.call-start = ((), (), s32[]{:S(2)}) async-start(), calls=%async_computation.18 | async-start | bytes 12976128 | tf_op jit(solution)/shard_map/reduce_scatter | solution.py:249
  779.7 910.1 %reduce-scatter.15.cloned.1.call-start = ((), (), s32[]{:S(2)}) async-start(), calls=%async_computation.20 | async-start | bytes 4325376 | tf_op jit(solution)/shard_map/reduce_scatter | solution.py:253
  784.5 0.7 copy-start.28
  784.5 1064.2 %reduce-scatter.13.cloned.1.call-start = ((), (), s32[]{:S(2)}) async-start(), calls=%async_computation.19 | async-start | bytes 12976128 | tf_op jit(solution)/shard_map/reduce_scatter | solution.py:251
  795.8 0.7 copy-start.23
  839.4 18.3 copy-start.14
  839.4 18.3 copy-start.16
Sparse Core Ops, SparseCore 0:
  10.9 99.1 all-gather.6
  113.0 67.7 all-gather.8
  183.9 57.9 all-gather.10
  244.9 76.2 all-gather.12
  324.2 76.0 all-gather.14
  428.6 190.8 reduce-scatter.20
  621.8 229.7 reduce-scatter.22
  853.9 183.4 reduce-scatter.16
  1039.7 183.4 reduce-scatter.18
  1229.1 155.7 reduce-scatter.8
  1392.0 154.4 reduce-scatter.10
  1549.2 140.5 reduce-scatter.14
  1696.4 152.3 reduce-scatter.12
where the time goes:
time: 1860 us
  waiting for transfers between devices  1220 us (66%)
  blocking collectives  215 us (12%)
  matrix products  205 us (11%)
  local copies, waits for them, and re-layouts  94.3 us (5%)
  other arithmetic  94.2 us (5%)
    reduce_scatter x1, waiting for transfers between devices, per_device(): lax.psum_scatter(up_right, ('dp', 'seq'), scatter_dimension=0, tiled=True)  186 us
    reduce_scatter x1, waiting for transfers between devices, per_device(): lax.psum_scatter(up_left, ('dp', 'seq'), scatter_dimension=0, tiled=True)  177 us
    reduce_scatter x1, waiting for transfers between devices, per_device(): lax.psum_scatter(ada_right, ('dp', 'seq'), scatter_dimension=0, tiled=True)  162 us
    reduce_scatter x1, waiting for transfers between devices, per_device(): lax.psum_scatter(ada_left, ('dp', 'seq'), scatter_dimension=0, tiled=True)  160 us
    reduce_scatter x1, waiting for transfers between devices, per_device(): lax.psum_scatter(grad_qkv_w, ('dp', 'seq'), scatter_dimension=0, tiled=True)  159 us
    reduce_scatter x1, waiting for transfers between devices, per_device(): lax.psum_scatter(grad_proj_w, ('dp', 'seq'), scatter_dimension=0, tiled=T...  141 us
    all_to_all x1, waiting for transfers between devices, per_device(): lax.all_to_all(grad_mixed, 'seq', split_axis=1, concat_axis=3, tiled=True)  91.6 us
    unnamed x2, blocking collectives  83.3 us
  transfers between devices with their start and end apart: 16, of which 10 were waited for; matrix products, arithmetic and copies ran while one was open for 21% of the time, Pallas kernels for 0%

commit v1 on v0

v1 whole, which is shorter than its diff:
```python
import functools
import math

import jax
import jax.numpy as jnp
from jax import lax
from jax.experimental import pallas as pl
from jax.experimental.pallas import tpu as pltpu
from jax.sharding import PartitionSpec as P

H = 16


norm_eps = 1e-06
exact_mode = lax.Precision.HIGHEST


def normalize_rows(values):
    centre = values - jnp.mean(values, axis=-1, keepdims=True)
    inv_std = lax.rsqrt(jnp.mean(centre * centre, axis=-1, keepdims=True) + norm_eps)
    return (centre * inv_std, inv_std)


def norm_back(grad_norm, normed, inv_std):
    first_mean = jnp.mean(grad_norm, axis=-1, keepdims=True)
    second_mean = jnp.mean(grad_norm * normed, axis=-1, keepdims=True)
    return inv_std * (grad_norm - first_mean - normed * second_mean)


def gelu_tanh(inputs):
    return jax.nn.gelu(inputs, approximate=True)


NT = (((1,), (1,)), ((), ()))
TN = (((0,), (0,)), ((), ()))
LANES = 128


def mm(left, right, dims=None):
    if dims is None:
        return jnp.dot(left, right, preferred_element_type=jnp.float32)
    return lax.dot_general(left, right, dims, preferred_element_type=jnp.float32)


def head_masks(head_dim):
    lane = lax.broadcasted_iota(jnp.int32, (1, LANES), 1)
    return [lane // head_dim == one for one in range(LANES // head_dim)]


def attend_kernel(head_dim, block, qkv_ref, out_ref):
    masks = head_masks(head_dim)
    factor = jnp.bfloat16(1.0 / math.sqrt(head_dim))

    def step(index, carry):
        rows = pl.ds(pl.multiple_of(index * block, block), block)
        queries = qkv_ref[0, 0, rows, :] * factor
        output = jnp.zeros((block, LANES), jnp.float32)
        for mask in masks:
            own = jnp.where(mask, queries, jnp.zeros_like(queries))
            scores = mm(own, qkv_ref[0, 1], NT)
            expo = jnp.exp(scores - jnp.max(scores, axis=1, keepdims=True))
            inverse = 1.0 / jnp.sum(expo, axis=1, keepdims=True)
            probs_low = (expo * inverse).astype(jnp.bfloat16)
            output = jnp.where(mask, mm(probs_low, qkv_ref[0, 2]), output)
        out_ref[0, rows, :] = output.astype(jnp.bfloat16)
        return carry

    lax.fori_loop(0, qkv_ref.shape[2] // block, step, 0)


def attend_back_kernel(head_dim, block, qkv_ref, cot_ref, out_ref, keys_acc, values_acc):
    masks = head_masks(head_dim)
    factor = jnp.bfloat16(1.0 / math.sqrt(head_dim))
    keys_acc[...] = jnp.zeros_like(keys_acc)
    values_acc[...] = jnp.zeros_like(values_acc)

    def step(index, carry):
        rows = pl.ds(pl.multiple_of(index * block, block), block)
        queries = qkv_ref[0, 0, rows, :] * factor
        cot = cot_ref[0, rows, :]
        grad_queries = jnp.zeros((block, LANES), jnp.float32)
        for mask in masks:
            own = jnp.where(mask, queries, jnp.zeros_like(queries))
            own_cot = jnp.where(mask, cot, jnp.zeros_like(cot))
            scores = mm(qkv_ref[0, 1], own, NT)
            expo = jnp.exp(scores - jnp.max(scores, axis=0, keepdims=True))
            probs = expo * (1.0 / jnp.sum(expo, axis=0, keepdims=True))
            grad_probs = mm(qkv_ref[0, 2], own_cot, NT)
            inner = jnp.sum(probs * grad_probs, axis=0, keepdims=True)
            grad_scores = (probs * (grad_probs - inner)).astype(jnp.bfloat16)
            values_acc[...] += mm(probs.astype(jnp.bfloat16), own_cot)
            keys_acc[...] += mm(grad_scores, own)
            grad_queries = jnp.where(mask, mm(grad_scores, qkv_ref[0, 1], TN), grad_queries)
        grad_queries = grad_queries * (1.0 / math.sqrt(head_dim))
        out_ref[0, 0, rows, :] = grad_queries.astype(jnp.bfloat16)
        return carry

    lax.fori_loop(0, qkv_ref.shape[2] // block, step, 0)
    out_ref[0, 1] = keys_acc[...].astype(jnp.bfloat16)
    out_ref[0, 2] = values_acc[...].astype(jnp.bfloat16)


def attend(heads, head_dim):
    groups, _, length, width = heads.shape
    work = groups * width * length * length
    return pl.pallas_call(
        functools.partial(attend_kernel, head_dim, min(length, 256)),
        out_shape=jax.ShapeDtypeStruct((groups, length, width), jnp.bfloat16),
        grid=(groups, width // LANES),
        in_specs=[pl.BlockSpec((1, 3, length, LANES), lambda g, c: (g, 0, 0, c))],
        out_specs=pl.BlockSpec((1, length, LANES), lambda g, c: (g, 0, c)),
        compiler_params=pltpu.CompilerParams(vmem_limit_bytes=32 * 1024 * 1024),
        cost_estimate=pl.CostEstimate(
            flops=16 * work, bytes_accessed=8 * groups * length * width, transcendentals=0
        ),
    )(heads)


def attend_back(heads, grad_heads, head_dim):
    groups, _, length, width = heads.shape
    work = groups * width * length * length
    return pl.pallas_call(
        functools.partial(attend_back_kernel, head_dim, min(length, 256)),
        out_shape=jax.ShapeDtypeStruct(heads.shape, jnp.bfloat16),
        grid=(groups, width // LANES),
        in_specs=[
            pl.BlockSpec((1, 3, length, LANES), lambda g, c: (g, 0, 0, c)),
            pl.BlockSpec((1, length, LANES), lambda g, c: (g, 0, c)),
        ],
        out_specs=pl.BlockSpec((1, 3, length, LANES), lambda g, c: (g, 0, 0, c)),
        scratch_shapes=[pltpu.VMEM((length, LANES), jnp.float32)] * 2,
        compiler_params=pltpu.CompilerParams(vmem_limit_bytes=32 * 1024 * 1024),
        cost_estimate=pl.CostEstimate(
            flops=40 * work, bytes_accessed=14 * groups * length * width, transcendentals=0
        ),
    )(heads, grad_heads)


AXES = ("dp", "seq")
CORE_Y = (2, 1, 4, 8, 16)
CORE_X = (2, 4, 8, 1, 16)
CORE_Z = (2, 8, 4, 1, 16)


def axis_sizes():
    return lax.axis_size("dp"), lax.axis_size("seq")


def flat_index():
    return lax.axis_index("dp") * lax.axis_size("seq") + lax.axis_index("seq")


def swap(values, mask):
    dp_size, seq_size = axis_sizes()
    pairs = [(one, one ^ mask) for one in range(dp_size * seq_size)]
    return lax.ppermute(values, AXES, pairs)


def gather_small(values):
    dp_size, seq_size = axis_sizes()
    total = values[None]
    mask = 1
    while mask < dp_size * seq_size:
        other = swap(total, mask)
        upper = (flat_index() & mask) != 0
        total = jnp.concatenate(
            [jnp.where(upper, other, total), jnp.where(upper, total, other)], axis=0
        )
        mask *= 2
    return total


def sum_rows_by_latent(partial):
    dp_size, seq_size = axis_sizes()
    mask = dp_size * seq_size // 2
    total = partial
    while mask >= seq_size:
        half = total.shape[0] // 2
        bit = (flat_index() // mask) & 1
        sent = lax.dynamic_slice_in_dim(total, (1 - bit) * half, half, 0)
        kept = lax.dynamic_slice_in_dim(total, bit * half, half, 0)
        total = kept + swap(sent, mask)
        mask //= 2
    while mask >= 1:
        total = total + swap(total, mask)
        mask //= 2
    return total


def scatter_sum(grad, first_masks):
    dp_size, seq_size = axis_sizes()
    count = dp_size * seq_size
    rows, cols = grad.shape
    masks = []
    mask = count // 2
    while mask >= 1:
        masks.append(mask)
        mask //= 2
    order = [one for one in first_masks if one in masks]
    order += [one for one in masks if one not in order]
    total = grad.reshape([2] * len(masks) + [rows // count, cols])
    left = list(masks)
    for mask in order:
        axis = left.index(mask)
        left.pop(axis)
        bit = (flat_index() // mask) & 1
        sent = lax.dynamic_index_in_dim(total, 1 - bit, axis, keepdims=False)
        kept = lax.dynamic_index_in_dim(total, bit, axis, keepdims=False)
        total = kept.astype(jnp.float32) + swap(sent, mask).astype(jnp.float32)
        if left:
            total = total.astype(jnp.bfloat16)
    return total


def per_device(
    hidden_in,
    cond_in,
    ada_weight,
    ada_bias,
    qkv_weight,
    qv_bias,
    proj_weight,
    proj_bias,
    up_weight,
    up_bias,
    down_weight,
    down_bias,
    out_cot,
):
    groups, local_len, model_width = hidden_in.shape
    dp_size, seq_size = axis_sizes()
    count = dp_size * seq_size
    own_cond = ada_weight.shape[0]
    qkv_full = lax.all_gather(qkv_weight, AXES, axis=0, tiled=True)
    smalls = (ada_bias, qv_bias, proj_bias, up_bias, down_bias, cond_in.reshape(-1))
    packed = gather_small(jnp.concatenate(smalls))
    fulls = []
    offset = 0
    for one in smalls:
        width = one.shape[0]
        fulls.append(packed[:, offset : offset + width].reshape(-1))
        offset += width
    ada_bias_full, qv_bias_full, proj_bias_full, up_bias_full, down_bias_full, cond_copies = fulls
    cond_all = cond_copies.reshape(dp_size, seq_size, groups, -1)[:, 0]
    cond_all = cond_all.reshape(dp_size * groups, -1).astype(jnp.float32)
    cond_columns = lax.dynamic_slice_in_dim(cond_all, flat_index() * own_cond, own_cond, 1)
    cond_columns = jax.nn.silu(cond_columns).astype(jnp.bfloat16)
    proj_full = lax.all_gather(proj_weight, AXES, axis=0, tiled=True)
    up_full = lax.all_gather(up_weight, AXES, axis=0, tiled=True)
    down_full = lax.all_gather(down_weight, AXES, axis=0, tiled=True)
    row_count = groups * local_len
    cond_float = cond_in.astype(jnp.float32)
    modul = sum_rows_by_latent(
        jnp.dot(cond_columns, ada_weight, preferred_element_type=jnp.float32)
    ) + ada_bias_full.astype(jnp.float32)
    modul = modul.reshape(groups, 6, 1, model_width)
    shift_att = modul[:, 0]
    scale_att = modul[:, 1]
    gate_att = modul[:, 2]
    shift_mlp = modul[:, 3]
    scale_mlp = modul[:, 4]
    gate_mlp = modul[:, 5]
    source = hidden_in.astype(jnp.float32)
    normed_one, inv_one = normalize_rows(source)
    first_in = (normed_one * (1.0 + scale_att) + shift_att).astype(jnp.bfloat16)
    first_flat = first_in.reshape(row_count, model_width)
    qv_full = qv_bias_full.astype(jnp.float32)
    zero_bias = jnp.zeros((model_width,), jnp.float32)
    qkv_bias = jnp.concatenate([qv_full[:model_width], zero_bias, qv_full[model_width:]])
    mixed = jnp.dot(first_flat, qkv_full, preferred_element_type=jnp.float32) + qkv_bias
    mixed = mixed.astype(jnp.bfloat16).reshape(groups, local_len, 3, model_width)
    mixed = jnp.swapaxes(mixed, 1, 2)
    heads = lax.all_to_all(mixed, "seq", split_axis=3, concat_axis=2, tiled=True)
    head_dim = model_width // H
    attended = attend(heads, head_dim)
    back_tokens = lax.all_to_all(attended, "seq", split_axis=1, concat_axis=2, tiled=True)
    attended_flat = back_tokens.reshape(row_count, model_width)
    branch = jnp.dot(attended_flat, proj_full, preferred_element_type=jnp.float32)
    branch = branch + proj_bias_full.astype(jnp.float32)
    branch = branch.reshape(groups, local_len, model_width)
    middle = source + gate_att * branch
    normed_two, inv_two = normalize_rows(middle)
    second_in = (normed_two * (1.0 + scale_mlp) + shift_mlp).astype(jnp.bfloat16)
    second_flat = second_in.reshape(row_count, model_width)
    up_pre = jnp.dot(second_flat, up_full, preferred_element_type=jnp.float32) + up_bias_full.astype(
        jnp.float32
    )
    act_value, gelu_pull = jax.vjp(gelu_tanh, up_pre)
    act_low = act_value.astype(jnp.bfloat16)
    mlp_out = jnp.dot(act_low, down_full, preferred_element_type=jnp.float32) + down_bias_full.astype(
        jnp.float32
    )
    mlp_out = mlp_out.reshape(groups, local_len, model_width)
    result = (middle + gate_mlp * mlp_out).astype(jnp.bfloat16)
    grad_out = out_cot.astype(jnp.float32)
    grad_gate_mlp = jnp.sum(grad_out * mlp_out, axis=1)
    grad_mlp = (grad_out * gate_mlp).astype(jnp.bfloat16).reshape(row_count, model_width)
    grad_down_w = jnp.dot(act_low.T, grad_mlp, preferred_element_type=jnp.float32)
    own_down_w = scatter_sum(grad_down_w.astype(jnp.bfloat16), CORE_Y)
    grad_down_b = jnp.sum(grad_mlp.astype(jnp.float32), axis=0)
    grad_act = jnp.dot(grad_mlp, down_full.T, preferred_element_type=jnp.float32)
    grad_up = gelu_pull(grad_act)[0].astype(jnp.bfloat16)
    grad_up_w = jnp.dot(second_flat.T, grad_up, preferred_element_type=jnp.float32)
    own_up_w = scatter_sum(grad_up_w.astype(jnp.bfloat16), CORE_X)
    grad_up_b = jnp.sum(grad_up.astype(jnp.float32), axis=0)
    grad_second = jnp.dot(grad_up, up_full.T, preferred_element_type=jnp.float32).reshape(
        groups, local_len, model_width
    )
    grad_shift_mlp = jnp.sum(grad_second, axis=1)
    grad_scale_mlp = jnp.sum(grad_second * normed_two, axis=1)
    grad_middle = grad_out + norm_back(grad_second * (1.0 + scale_mlp), normed_two, inv_two)
    grad_gate_att = jnp.sum(grad_middle * branch, axis=1)
    grad_branch = (grad_middle * gate_att).astype(jnp.bfloat16).reshape(row_count, model_width)
    grad_proj_w = jnp.dot(attended_flat.T, grad_branch, preferred_element_type=jnp.float32)
    own_proj_w = scatter_sum(grad_proj_w.astype(jnp.bfloat16), CORE_Z)
    grad_proj_b = jnp.sum(grad_branch.astype(jnp.float32), axis=0)
    grad_attended = jnp.dot(grad_branch, proj_full.T, preferred_element_type=jnp.float32)
    grad_attended = grad_attended.astype(jnp.bfloat16).reshape(groups, local_len, model_width)
    grad_heads = lax.all_to_all(grad_attended, "seq", split_axis=2, concat_axis=1, tiled=True)
    grad_mixed = attend_back(heads, grad_heads, head_dim)
    grad_local = lax.all_to_all(grad_mixed, "seq", split_axis=2, concat_axis=3, tiled=True)
    grad_flat = jnp.swapaxes(grad_local, 1, 2).reshape(row_count, 3 * model_width)
    grad_qkv_w = jnp.dot(first_flat.T, grad_flat, preferred_element_type=jnp.float32)
    own_qkv_w = scatter_sum(grad_qkv_w.astype(jnp.bfloat16), CORE_Z)
    bias_total = jnp.sum(grad_flat.astype(jnp.float32), axis=0)
    grad_qv_b = jnp.concatenate([bias_total[:model_width], bias_total[2 * model_width :]])
    grad_first = jnp.dot(grad_flat, qkv_full.T, preferred_element_type=jnp.float32).reshape(
        groups, local_len, model_width
    )
    grad_shift_att = jnp.sum(grad_first, axis=1)
    grad_scale_att = jnp.sum(grad_first * normed_one, axis=1)
    grad_input = grad_middle + norm_back(grad_first * (1.0 + scale_att), normed_one, inv_one)
    grad_modul = jnp.stack(
        [
            grad_shift_att,
            grad_scale_att,
            grad_gate_att,
            grad_shift_mlp,
            grad_scale_mlp,
            grad_gate_mlp,
        ],
        axis=1,
    )
    grad_modul = grad_modul.reshape(groups, 6 * model_width)
    small_grads = (grad_qv_b, grad_proj_b, grad_up_b, grad_down_b, grad_modul.reshape(-1))
    gathered = gather_small(jnp.concatenate(small_grads))
    split_at = sum(one.shape[0] for one in small_grads[:-1])
    bias_sums = jnp.sum(gathered[:, :split_at], axis=0)
    modul_all = gathered[:, split_at:].reshape(dp_size, seq_size, groups, -1)
    modul_all = jnp.sum(modul_all, axis=1).reshape(dp_size * groups, -1)
    own_biases = []
    offset = 0
    for one in small_grads[:-1] + (jnp.sum(modul_all, axis=0),):
        width = one.shape[0]
        whole_bias = bias_sums[offset : offset + width] if offset < split_at else one
        offset += width
        own_width = width // count
        own_biases.append(
            lax.dynamic_slice_in_dim(whole_bias, flat_index() * own_width, own_width, 0)
        )
    cond_wide = cond_columns.astype(jnp.float32)
    own_ada_w = jnp.dot(cond_wide.T, modul_all, precision=exact_mode)
    cond_part = jnp.dot(modul_all, ada_weight.astype(jnp.float32).T, precision=exact_mode)
    cond_parts = gather_small(cond_part)
    cond_total = lax.dynamic_slice_in_dim(
        cond_parts, lax.axis_index("dp") * groups, groups, 1
    )
    cond_total = jnp.swapaxes(cond_total, 0, 1).reshape(groups, -1)
    silu_value, silu_pull = jax.vjp(jax.nn.silu, cond_float)
    grad_condition = silu_pull(cond_total)[0]
    return (
        result,
        grad_input,
        grad_condition,
        own_ada_w,
        own_biases[4],
        own_qkv_w,
        own_biases[0],
        own_proj_w,
        own_biases[1],
        own_up_w,
        own_biases[2],
        own_down_w,
        own_biases[3],
    )


def solution(mesh):
    placed = (
        P("dp", "seq", None),
        P("dp", None),
        P(("dp", "seq"), None),
        P(("dp", "seq")),
        P(("dp", "seq"), None),
        P(("dp", "seq")),
        P(("dp", "seq"), None),
        P(("dp", "seq")),
        P(("dp", "seq"), None),
        P(("dp", "seq")),
        P(("dp", "seq"), None),
        P(("dp", "seq")),
        P("dp", "seq", None),
    )
    return jax.shard_map(
        per_device,
        mesh=mesh,
        in_specs=placed,
        out_specs=(
            P("dp", "seq", None),
            P("dp", "seq", None),
            P("dp", None),
            P(("dp", "seq"), None),
            P(("dp", "seq")),
            P(("dp", "seq"), None),
            P(("dp", "seq")),
            P(("dp", "seq"), None),
            P(("dp", "seq")),
            P(("dp", "seq"), None),
            P(("dp", "seq")),
            P(("dp", "seq"), None),
            P(("dp", "seq")),
        ),
        check_vma=False,
    )
```

time: 1860 us -> 781 us (0.42)
  waiting for transfers between devices: 1220 us -> 308 us
  blocking collectives: 215 us -> 55.5 us
  matrix products: 205 us -> 102 us
  Pallas kernels: 0 us -> 65.4 us
  starting transfers between devices: 14.5 us -> 56.3 us
  other arithmetic: 94.2 us -> 62.5 us
    reduce_scatter x8 -> x0, waiting for transfers between devices: 985 us -> none  [the longest x1 186 us: per_device(): lax.psum_scatter(up_right, ('dp', 'seq'), scatter_dimension=0, tiled=True)]
    ppermute x0 -> x40, waiting for transfers between devices: none -> 190 us  [swap(): return lax.ppermute(values, AXES, pairs)]
    dot_general x12 -> x7, matrix products: 139 us -> 37.6 us  [the longest x1 16.6 us: per_device(): jnp.dot(grad_mlp, down_full.T, preferred_element_type=jnp.float32)]
    unnamed x2 -> x0, blocking collectives: 83.3 us -> none
    all_to_all x1, waiting for transfers between devices: 91.6 us -> 20.7 us  [per_device(): lax.all_to_all(grad_mixed, 'seq', split_axis=2, concat_axis=3, tiled=True)]
    all_gather x1 -> x0, blocking collectives: 70.7 us -> none  [per_device(): lax.all_gather(params[7], ('dp', 'seq'), axis=0, tiled=True)]
    pallas_call x0 -> x2, Pallas kernels: none -> 65.4 us  [the longest x1 42.6 us: attend_back(): pl.pallas_call(functools.partial(attend_back_kernel, head_dim, min(length...]
    ppermute x0 -> x40, starting transfers between devices: none -> 40.6 us  [swap(): return lax.ppermute(values, AXES, pairs)]
  transfers between devices with their start and end apart: 16 -> 47, of which waited for: 10 -> 34; matrix products, arithmetic and copies ran while one was open for 21% -> 26% of each run, Pallas kernels for 0% -> 8%
where the time goes in v1:
time: 781 us; the launch traced here: 774 us
  waiting for transfers between devices  308 us (39%)
  local copies, waits for them, and re-layouts  108 us (14%)
  matrix products  102 us (13%)
  Pallas kernels  65.4 us (8%)
  other arithmetic  62.5 us (8%)
  starting transfers between devices  56.3 us (7%)
  blocking collectives  55.5 us (7%)
  between operations  15.1 us (2%)
    ppermute x40, waiting for transfers between devices, swap(): return lax.ppermute(values, AXES, pairs)  190 us
    all_gather x1, waiting for transfers between devices, per_device(): down_full = lax.all_gather(down_weight, AXES, axis=0, tiled=True)  62.1 us
    all_to_all x1, blocking collectives, per_device(): lax.all_to_all(mixed, 'seq', split_axis=3, concat_axis=2, tiled=True)  55.5 us
    pallas_call x1, Pallas kernels, attend_back(): pl.pallas_call(functools.partial(attend_back_kernel, head_dim, min(length...  42.6 us
    ppermute x40, starting transfers between devices, swap(): return lax.ppermute(values, AXES, pairs)  40.6 us
    unnamed x134, local copies, waits for them, and re-layouts  31.8 us
    pallas_call x1, Pallas kernels, attend(): pl.pallas_call(functools.partial(attend_kernel, head_dim, min(length, 256...  22.9 us
    all_to_all x1, waiting for transfers between devices, per_device(): lax.all_to_all(grad_mixed, 'seq', split_axis=2, concat_axis=3, tiled=True)  20.7 us
  transfers between devices with their start and end apart: 47, of which 34 were waited for; matrix products, arithmetic and copies ran while one was open for 26% of the time, Pallas kernels for 8%

profile of v1, /device:TPU:0, one launch (start us, length us, event | category | flops | bytes accessed | tf_op | source)
XLA Modules:
  0.0 773.8 jit_solution(5016156147307073306)
XLA Ops:
  10.2 3.4 concatenate.54
  13.6 3.0 collective-permute-start
  27.5 3.0 collective-permute-start.4
  31.0 2.6 collective-permute-done.4
  36.6 11.6 %collective-permute-done.5 = f32[8,6144]{1,0:T(8,128)S(1)} collective-permute-done((f32[8,6144]{1,0:T(8,128)S(1)}, f32[8,6144]{1,0:T(8,128)S(1)}, u32[]{:S(2)}, u32[]{:S(2)}) %collective-permute-start.5) | collective-permute-done | bytes 196640 | tf_op jit(solution)/shard_map/ppermute | solution.py:156
  48.4 7.1 collective-permute-done.6
  56.4 3.2 collective-permute-done.7
  65.9 19.5 %all-gather.5.cloned.1.call-done = bf16[1024,3072]{1,0:T(8,128)(2,1)} async-done(((bf16[32,3072]{1,0:T(8,128)(2,1)}), bf16[1024,3072]{1,0:T(8,128)(2,1)}) %all-gather.5.cloned.1.call-update) | async-done | bytes 6291472 | tf_op jit(solution)/shard_map/all_gather | solution.py:234
  85.4 7.9 %add_convert_fusion = bf16[512,3072]{1,0:T(8,128)(2,1)} fusion(bf16[1024,3072]{1,0:T(8,128)(2,1)} %all-gather.5.cloned.1.call-done, f32[3072]{0:T(1024)S(1)} %pad_maximum_fusion.13, bf16[1,512,1024]{2,1,0:T(8,128)(2,1)S(1)} %copy-done.5, f32[1024]{0:T(1024)S(1)} %bitcast.292, f32[1024]{0:T(1024)S(1)} %bitcast.268, f32[512]{0:T(512)S(1)} %add_rsqrt_fusion.1, ...), kind=kOutput, calls=%fused_computation.20 | convolution fusion | flops 3227516928 | bytes 10510336 | tf_op jit(solution)/shard_map/dot_general | solution.py:270
  93.3 3.2 copy.83
  96.5 2.7 copy.84
  99.2 55.5 %all_to_all.69 = bf16[1,3,512,1024]{2,1,0,3:T(4,128)(2,1)S(1)} all-to-all(bf16[1,3,512,1024]{2,1,0,3:T(4,128)(2,1)S(1)} %copy.84), channel_id=1, replica_groups=mesh['dp'=16,'seq'=2] {'seq'}, dimensions={3} | all-to-all | bytes 6291456 | tf_op jit(solution)/shard_map/all_to_all | solution.py:273
  157.1 3.3 copy.86
  160.4 22.9 %shard_map.228 = bf16[1,1024,512]{2,1,0:T(8,128)(2,1)S(1)} custom-call(bf16[1,3,1024,512]{3,2,1,0:T(8,128)(2,1)S(1)} %bitcast.245), custom_call_target="tpu_custom_call" | custom-call | flops 8589934592 | bytes 4194304 | tf_op jit(solution)/shard_map/pallas_call | solution.py:106
  183.3 2.9 copy.131
  186.8 9.0 %reduce.33 = bf16[1024,512]{1,0:T(8,128)(2,1)} reduce(bf16[1024,1,512]{2,1,0:T(2,128)(2,1)} %bitcast.257, bf16[]{:T(256)} %broadcast.173), dimensions={1}, to_apply=%bitcast.243.reduce_sub_computation | reduce | bytes 2097154
  195.8 2.8 reshape.362
  198.6 4.7 all-to-all-start.1
  210.2 14.1 %all-to-all-done.1 = bf16[2,2,131072]{2,1,0:T(2,128)(2,1)} async-done(((bf16[2,2,131072]{2,1,0:T(2,128)(2,1)}), bf16[2,2,131072]{2,1,0:T(2,128)(2,1)}, u32[]{:S(2)}, u32[]{:S(2)}) %all-to-all-start.1) | async-done | bytes 1048608 | tf_op jit(solution)/shard_map/all_to_all | solution.py:276
  224.3 2.9 reshape.363
  227.2 2.9 copy.103
  232.3 4.9 fusion.81
  239.5 12.0 %fusion.74 = f32[512,4096]{1,0:T(8,128)} fusion(bf16[1024,4096]{1,0:T(8,128)(2,1)} %all-gather.9.cloned.1.call-done, f32[1,512,1024]{2,1,0:T(8,128)} %copy-done.18, f32[1024]{0:T(1024)} %bitcast.294, f32[1024]{0:T(1024)S(1)} %bitcast.275, f32[512]{0:T(512)} %add_rsqrt_fusion, f32[512]{0:T(512)S(1)} %broadcast_multiply_fusion.4), kind=kOutput, calls=%fused_computation.237 | convolution fusion | flops 4297588736 | bytes 18886656 | tf_op jit(solution)/shard_map/dot_general | solution.py:285
  251.5 62.1 %all-gather.11.cloned.1.call-done = bf16[4096,1024]{1,0:T(8,128)(2,1)} async-done(((bf16[128,1024]{1,0:T(8,128)(2,1)}), bf16[4096,1024]{1,0:T(8,128)(2,1)}) %all-gather.11.cloned.1.call-update) | async-done | bytes 8388624 | tf_op jit(solution)/shard_map/all_gather | solution.py:250
  313.6 16.6 %convert_reduce_fusion = (f32[4096]{0:T(1024)}, bf16[512,4096]{1,0:T(8,128)(2,1)}) fusion(f32[512,4096]{1,0:T(8,128)} %fusion.74, f32[4096]{0:T(1024)} %bitcast_convert_fusion, bf16[4096,1024]{1,0:T(8,128)(2,1)} %all-gather.11.cloned.1.call-done, bf16[1,512,1024]{2,1,0:T(8,128)(2,1)} %param.25, f32[1024]{0:T(1024)S(1)} %bitcast.281), kind=kOutput, calls=%fused_computation.13 | convolution fusion | flops 4344770560 | bytes 22056960 | tf_op jit(solution)/shard_map/dot_general | solution.py:301
  330.2 8.0 %fusion.32 = (f32[1024]{0:T(1024)}, f32[512]{0:T(512)S(1)}, f32[512,1024]{1,0:T(8,128)S(1)}) fusion(f32[1,512,1024]{2,1,0:T(8,128)S(1)} %copy-done.19, f32[512]{0:T(512)S(1)} %copy-done.56, f32[512]{0:T(512)S(1)} %broadcast_multiply_fusion.4, f32[1024]{0:T(1024)S(1)} %bitcast.276, bf16[512,4096]{1,0:T(8,128)(2,1)} %get-tuple-element.89, ...), kind=kOutput, calls=%fused_computation.63 | convolution fusion | flops 4298635776 | bytes 16791552 | tf_op jit(solution)/shard_map/dot_general | solution.py:306
  339.5 12.7 %fusion.28 = (f32[1024]{0:T(1024)}, bf16[1,512,1024]{2,1,0:T(8,128)(2,1)}, f32[1024]{0:T(1024)}, f32[1,512,1024]{2,1,0:T(8,128)S(1)}) fusion(bf16[1,512,1024]{2,1,0:T(8,128)(2,1)S(1)} %copy-done.25, f32[1024]{0:T(1024)S(1)} %copy-done.52, f32[1,512,1024]{2,1,0:T(8,128)S(1)} %copy-done.19, f32[1024]{0:T(1024)S(1)} %bitcast.282, ...), kind=kOutput, calls=%fused_computation.55 | convolution fusion | flops 4325373952 | bytes 27312128 | tf_op jit(solution)/shard_map/dot_general | solution.py:290
  357.7 6.1 copy.89
  363.9 9.0 %reduce.34 = bf16[1024,512]{1,0:T(8,128)(2,1)} reduce(bf16[1024,1,512]{2,1,0:T(2,128)(2,1)} %bitcast.258, bf16[]{:T(256)} %broadcast.173), dimensions={1}, to_apply=%bitcast.211.reduce_sub_computation | reduce | bytes 2097154
  372.9 2.6 reshape.364
  375.5 4.6 all-to-all-start.2
  380.2 13.9 %convolution_convert_fusion = bf16[4096,1024]{1,0:T(8,128)(2,1)} fusion(bf16[1,512,1024]{2,1,0:T(8,128)(2,1)} %param.25, f32[1024]{0:T(1024)S(1)} %bitcast.283, f32[512,4096]{1,0:T(8,128)} %fusion.74, f32[4096]{0:T(1024)} %bitcast_convert_fusion), kind=kOutput, calls=%fused_computation.15 | convolution fusion | flops 4321705984 | bytes 17846272 | tf_op jit(solution)/shard_map/dot_general | solution.py:298
  397.8 3.1 reshape.365
  401.0 2.8 copy.104
  407.3 42.6 %shard_map.229 = bf16[1,3,1024,512]{3,2,1,0:T(8,128)(2,1)S(1)} custom-call(bf16[1,3,1024,512]{3,2,1,0:T(8,128)(2,1)S(1)} %bitcast.246, bf16[1,1024,512]{2,1,0:T(8,128)(2,1)S(1)} %bitcast.247), custom_call_target="tpu_custom_call" | custom-call | flops 21474836480 | bytes 7340032 | tf_op jit(solution)/shard_map/pallas_call | solution.py:122
  449.9 4.6 copy.91
  454.5 6.2 all-to-all-start.3
  460.8 7.6 convolution_convert_fusion.1
  472.4 2.9 constant_dynamic-slice_fusion.3
  477.6 7.6 collective-permute-done.26
  488.4 20.7 %all-to-all-done.3 = bf16[1,3,1024,512]{3,1,0,2:T(4,128)(2,1)} async-done(((bf16[1,3,1024,512]{3,1,0,2:T(4,128)(2,1)}), bf16[1,3,1024,512]{3,1,0,2:T(4,128)(2,1)}, u32[]{:S(2)}, u32[]{:S(2)}) %all-to-all-start.3) | async-done | bytes 3145760 | tf_op jit(solution)/shard_map/all_to_all | solution.py:321
  509.1 3.0 copy.92
  512.1 3.0 copy.93
  517.9 7.7 fusion.25
  536.7 3.3 collective-permute-done.10
  544.1 2.9 collective-permute-done.28
  552.2 7.0 constant_dynamic-slice_fusion.1
  559.1 2.7 copy.127
  564.6 4.5 convolution_convert_fusion.2
  572.0 34.1 %collective-permute-done.14 = f32[16,14336]{1,0:T(8,128)S(1)} collective-permute-done((f32[16,14336]{1,0:T(8,128)S(1)}, f32[16,14336]{1,0:T(8,128)S(1)}, u32[]{:S(2)}, u32[]{:S(2)}) %collective-permute-start.14) | collective-permute-done | bytes 917536 | tf_op jit(solution)/shard_map/ppermute | solution.py:156
  611.3 2.8 reduce_sum.207
  628.2 4.1 collective-permute-done.18
  636.6 2.6 collective-permute-done.19
  640.0 5.0 fusion.8
  647.3 4.3 fusion.7
  655.0 34.8 %collective-permute-done.31 = bf16[2,2,2,32,4096]{4,3,0,2,1:T(8,128)(2,1)S(1)} collective-permute-done((bf16[2,2,2,32,4096]{4,3,0,2,1:T(8,128)(2,1)S(1)}, bf16[2,2,2,32,4096]{4,3,0,2,1:T(8,128)(2,1)S(1)}, u32[]{:S(2)}, u32[]{:S(2)}) %collective-permute-start.31) | collective-permute-done | bytes 2097184 | tf_op jit(solution)/shard_map/ppermute | solution.py:156
  690.8 5.5 collective-permute-done.36
  700.4 11.5 %collective-permute-done.32 = bf16[2,2,32,4096]{3,2,0,1:T(8,128)(2,1)S(1)} collective-permute-done((bf16[2,2,32,4096]{3,2,0,1:T(8,128)(2,1)S(1)}, bf16[2,2,32,4096]{3,2,0,1:T(8,128)(2,1)S(1)}, u32[]{:S(2)}, u32[]{:S(2)}) %collective-permute-start.32) | collective-permute-done | bytes 1048608 | tf_op jit(solution)/shard_map/ppermute | solution.py:156
  713.4 10.3 %collective-permute-done.37 = bf16[2,2,128,1024]{3,2,0,1:T(8,128)(2,1)S(1)} collective-permute-done((bf16[2,2,128,1024]{3,2,0,1:T(8,128)(2,1)S(1)}, bf16[2,2,128,1024]{3,2,0,1:T(8,128)(2,1)S(1)}, u32[]{:S(2)}, u32[]{:S(2)}) %collective-permute-start.37) | collective-permute-done | bytes 1048608 | tf_op jit(solution)/shard_map/ppermute | solution.py:156
  724.3 11.1 %collective-permute-done.22 = bf16[2,2,32,3072]{3,2,0,1:T(8,128)(2,1)S(1)} collective-permute-done((bf16[2,2,32,3072]{3,2,0,1:T(8,128)(2,1)S(1)}, bf16[2,2,32,3072]{3,2,0,1:T(8,128)(2,1)S(1)}, u32[]{:S(2)}, u32[]{:S(2)}) %collective-permute-start.22) | collective-permute-done | bytes 786464 | tf_op jit(solution)/shard_map/ppermute | solution.py:156
  740.4 3.1 collective-permute-done.23
  744.8 12.4 %collective-permute-done.34 = bf16[32,4096]{1,0:T(8,128)(2,1)S(1)} collective-permute-done((bf16[32,4096]{1,0:T(8,128)(2,1)S(1)}, bf16[32,4096]{1,0:T(8,128)(2,1)S(1)}, u32[]{:S(2)}, u32[]{:S(2)}) %collective-permute-start.34) | collective-permute-done | bytes 262176 | tf_op jit(solution)/shard_map/ppermute | solution.py:156
  758.0 4.8 collective-permute-done.39
  763.7 2.5 collective-permute-done.24
  (334 shorter events, 136.7 us)
Async XLA Ops:
  7.2 26.6 %copy-start = (bf16[32,6144]{1,0:T(8,128)(2,1)S(1)}, bf16[32,6144]{1,0:T(8,128)(2,1)}, u32[]{:S(2)}) copy-start(bf16[32,6144]{1,0:T(8,128)(2,1)} %param.15) | copy-start | bytes 1179652
  7.2 23.3 %copy-start.5 = (bf16[1,512,1024]{2,1,0:T(8,128)(2,1)S(1)}, bf16[1,512,1024]{2,1,0:T(8,128)(2,1)}, u32[]{:S(2)}) copy-start(bf16[1,512,1024]{2,1,0:T(8,128)(2,1)} %param.13) | copy-start | bytes 3145732
  7.2 78.2 %all-gather.5.cloned.1.call-start = ((), (), s32[]{:S(2)}) async-start(), calls=%async_computation.4 | async-start | bytes 6488064 | tf_op jit(solution)/shard_map/all_gather | solution.py:234
  7.9 224.4 %all-gather.7.cloned.1.call-start = ((), (), s32[]{:S(2)}) async-start(), calls=%async_computation.5 | async-start | bytes 2162688 | tf_op jit(solution)/shard_map/all_gather | solution.py:248
  8.7 230.8 %all-gather.9.cloned.1.call-start = ((), (), s32[]{:S(2)}) async-start(), calls=%async_computation.6 | async-start | bytes 8650752 | tf_op jit(solution)/shard_map/all_gather | solution.py:249
  9.4 304.2 %all-gather.11.cloned.1.call-start = ((), (), s32[]{:S(2)}) async-start(), calls=%async_computation.7 | async-start | bytes 8650752 | tf_op jit(solution)/shard_map/all_gather | solution.py:250
  13.6 4.6 collective-permute-start
  18.3 1.2 collective-permute-start.1
  19.6 3.8 collective-permute-start.2
  23.4 4.0 collective-permute-start.3
  25.5 59.9 %copy-start.31 = (f32[512]{0:T(512)}, f32[512]{0:T(512)S(1)}, u32[]{:S(2)}) copy-start(f32[512]{0:T(512)S(1)} %broadcast_multiply_fusion.5) | copy-start | bytes 6148
  27.5 6.1 collective-permute-start.4
  33.6 51.8 %copy-start.21 = (bf16[16,1472]{1,0:T(8,128)(2,1)}, bf16[16,1472]{1,0:T(8,128)(2,1)S(1)}, u32[]{:S(2)}) copy-start(bf16[16,1472]{1,0:T(8,128)(2,1)S(1)} %get-tuple-element.57) | copy-start | bytes 141316
  33.6 51.8 %copy-start.22 = (bf16[16,1472]{1,0:T(8,128)(2,1)}, bf16[16,1472]{1,0:T(8,128)(2,1)S(1)}, u32[]{:S(2)}) copy-start(bf16[16,1472]{1,0:T(8,128)(2,1)S(1)} %get-tuple-element.58) | copy-start | bytes 141316
  33.8 22.6 %copy-start.27 = (f32[16,1,1,32]{3,1,0,2:T(1,128)}, f32[16,1,1,32]{3,1,0,2:T(1,128)S(1)}, u32[]{:S(2)}) copy-start(f32[16,1,1,32]{3,1,0,2:T(1,128)S(1)} %fusion.65) | copy-start | bytes 6148
  34.1 14.1 %collective-permute-start.5 = (f32[8,6144]{1,0:T(8,128)S(1)}, f32[8,6144]{1,0:T(8,128)S(1)}, u32[]{:S(2)}, u32[]{:S(2)}) collective-permute-start(f32[8,6144]{1,0:T(8,128)S(1)} %constant_dynamic-slice_fusion.11), channel_id=1, source_target_pairs={{0,16},{1,17},{2,18},{3,19},{4,20},{5,21},{6,22},{7,23},{8,24},{9,... | collective-permute-start | bytes 589832 | tf_op jit(solution)/shard_map/ppermute | solution.py:156
  36.6 48.8 %copy-start.45 = (f32[512]{0:T(512)}, f32[512]{0:T(512)S(1)}, u32[]{:S(2)}) copy-start(f32[512]{0:T(512)S(1)} %add_rsqrt_fusion.1) | copy-start | bytes 6148
  48.2 7.2 collective-permute-start.6
  55.5 4.2 collective-permute-start.7
  59.7 1.3 collective-permute-start.8
  61.0 4.2 collective-permute-start.9
  65.9 19.5 %copy-start.29 = (f32[1,1,1,1024]{3,1,2,0:T(1,128)}, f32[1,1,1,1024]{3,1,2,0:T(1,128)S(1)}, u32[]{:S(2)}) copy-start(f32[1,1,1,1024]{3,1,2,0:T(1,128)S(1)} %get-tuple-element.71) | copy-start | bytes 12292
  65.9 19.5 %copy-start.49 = (f32[1,1,1,1024]{3,1,2,0:T(1,128)}, f32[1,1,1,1024]{3,1,2,0:T(1,128)S(1)}, u32[]{:S(2)}) copy-start(f32[1,1,1,1024]{3,1,2,0:T(1,128)S(1)} %get-tuple-element.70) | copy-start | bytes 12292
  198.6 25.7 %all-to-all-start.1 = ((bf16[2,2,131072]{2,1,0:T(2,128)(2,1)}), bf16[2,2,131072]{2,1,0:T(2,128)(2,1)}, u32[]{:S(2)}, u32[]{:S(2)}) async-start(bf16[2,2,131072]{2,1,0:T(2,128)(2,1)} %reshape.362), calls=%async_computation.1 | async-start | bytes 2097152 | tf_op jit(solution)/shard_map/all_to_all | solution.py:276
  237.2 93.0 %copy-start.42 = (f32[512]{0:T(512)}, f32[512]{0:T(512)S(1)}, u32[]{:S(2)}) copy-start(f32[512]{0:T(512)S(1)} %broadcast_multiply_fusion.4) | copy-start | bytes 6148
  239.5 74.1 %copy-start.34 = (f32[1,1,1,1024]{3,1,2,0:T(1,128)S(1)}, f32[1,1,1,1024]{3,1,2,0:T(1,128)}, u32[]{:S(2)}) copy-start(f32[1,1,1,1024]{3,1,2,0:T(1,128)} %get-tuple-element.67) | copy-start | bytes 12292
  313.6 16.6 %copy-start.19 = (f32[1,512,1024]{2,1,0:T(8,128)S(1)}, f32[1,512,1024]{2,1,0:T(8,128)}, u32[]{:S(2)}) copy-start(f32[1,512,1024]{2,1,0:T(8,128)} %copy-done.18) | copy-start | bytes 6291460
  313.6 16.6 %copy-start.56 = (f32[512]{0:T(512)S(1)}, f32[512]{0:T(512)}, u32[]{:S(2)}) copy-start(f32[512]{0:T(512)} %add_rsqrt_fusion) | copy-start | bytes 6148
  313.6 16.6 %copy-start.58 = (bf16[1024,4096]{1,0:T(8,128)(2,1)S(1)}, bf16[1024,4096]{1,0:T(8,128)(2,1)}, u32[]{:S(2)}) copy-start(bf16[1024,4096]{1,0:T(8,128)(2,1)} %all-gather.9.cloned.1.call-done) | copy-start | bytes 25165828
  330.2 8.4 %copy-start.60 = (f32[512,1024]{1,0:T(8,128)S(1)}, f32[512,1024]{1,0:T(8,128)}, u32[]{:S(2)}) copy-start(f32[512,1024]{1,0:T(8,128)} %get-tuple-element.85) | copy-start | bytes 6291460
  375.5 22.3 %all-to-all-start.2 = ((bf16[2,2,131072]{2,1,0:T(2,128)(2,1)}), bf16[2,2,131072]{2,1,0:T(2,128)(2,1)}, u32[]{:S(2)}, u32[]{:S(2)}) async-start(bf16[2,2,131072]{2,1,0:T(2,128)(2,1)} %reshape.364), calls=%async_computation.2 | async-start | bytes 2097152 | tf_op jit(solution)/shard_map/all_to_all | solution.py:319
  380.2 13.9 %copy-start.24 = (bf16[512,1024]{1,0:T(8,128)(2,1)S(1)}, bf16[512,1024]{1,0:T(8,128)(2,1)}, u32[]{:S(2)}) copy-start(bf16[512,1024]{1,0:T(8,128)(2,1)} %copy-done.23) | copy-start | bytes 3145732
  380.2 13.9 %copy-start.26 = (bf16[1,512,2,512]{1,3,2,0:T(8,128)(2,1)S(1)}, bf16[1,512,2,512]{1,3,2,0:T(8,128)(2,1)}, u32[]{:S(2)}) copy-start(bf16[1,512,2,512]{1,3,2,0:T(8,128)(2,1)} %copy.88) | copy-start | bytes 3145732
  397.5 70.9 %collective-permute-start.25 = (bf16[2,2,2,2,32,1024]{5,4,0,3,2,1:T(8,128)(2,1)}, bf16[2,2,2,2,32,1024]{5,4,0,3,2,1:T(8,128)(2,1)}, u32[]{:S(2)}, u32[]{:S(2)}) collective-permute-start(bf16[2,2,2,2,32,1024]{5,4,0,3,2,1:T(8,128)(2,1)} %bitcast.242), channel_id=1, source_target_pairs={{0,2},{1,3},{2,0},{3,1},{4,6},{5,7},{6,4},{7,5},{8,10},{9,11},{10,... | collective-permute-start | bytes 3145736 | tf_op jit(solution)/shard_map/ppermute | solution.py:156
  454.5 54.6 %all-to-all-start.3 = ((bf16[1,3,1024,512]{3,1,0,2:T(4,128)(2,1)}), bf16[1,3,1024,512]{3,1,0,2:T(4,128)(2,1)}, u32[]{:S(2)}, u32[]{:S(2)}) async-start(bf16[1,3,1024,512]{3,1,0,2:T(4,128)(2,1)} %copy.91), calls=%async_computation.3 | async-start | bytes 8388608 | tf_op jit(solution)/shard_map/all_to_all | solution.py:321
  470.9 14.3 %collective-permute-start.26 = (bf16[2,2,2,32,1024]{4,3,0,2,1:T(8,128)(2,1)}, bf16[2,2,2,32,1024]{4,3,0,2,1:T(8,128)(2,1)S(1)}, u32[]{:S(2)}, u32[]{:S(2)}) collective-permute-start(bf16[2,2,2,32,1024]{4,3,0,2,1:T(8,128)(2,1)} %dynamic-slice_bitcast_fusion.8), channel_id=1, source_target_pairs={{0,8},{1,9},{2,10},{3,11},{4,12},{5,13},{6,14},{7,15},{8,0},{9,1},... | collective-permute-start | bytes 1572872 | tf_op jit(solution)/shard_map/ppermute | solution.py:156
  477.6 162.3 %collective-permute-start.30 = (bf16[2,2,2,2,32,4096]{5,4,0,3,1,2:T(8,128)(2,1)}, bf16[2,2,2,2,32,4096]{5,4,0,3,1,2:T(8,128)(2,1)}, u32[]{:S(2)}, u32[]{:S(2)}) collective-permute-start(bf16[2,2,2,2,32,4096]{5,4,0,3,1,2:T(8,128)(2,1)} %bitcast.240), channel_id=1, source_target_pairs={{0,2},{1,3},{2,0},{3,1},{4,6},{5,7},{6,4},{7,5},{8,10},{9,11},{10,... | collective-permute-start | bytes 12582920 | tf_op jit(solution)/shard_map/ppermute | solution.py:156
  486.9 48.6 %collective-permute-start.27 = (bf16[2,2,32,1024]{3,2,0,1:T(8,128)(2,1)}, bf16[2,2,32,1024]{3,2,0,1:T(8,128)(2,1)}, u32[]{:S(2)}, u32[]{:S(2)}) collective-permute-start(bf16[2,2,32,1024]{3,2,0,1:T(8,128)(2,1)} %dynamic-slice_bitcast_fusion.12), channel_id=1, source_target_pairs={{0,4},{1,5},{2,6},{3,7},{4,0},{5,1},{6,2},{7,3},{8,12},{9,13},{10,... | collective-permute-start | bytes 786440 | tf_op jit(solution)/shard_map/ppermute | solution.py:156
  535.5 4.4 collective-permute-start.10
  541.0 1.4 collective-permute-start.11
  541.1 6.0 collective-permute-start.28
  542.6 7.7 collective-permute-start.12
  547.1 14.8 %collective-permute-start.29 = (bf16[32,1024]{1,0:T(8,128)(2,1)S(1)}, bf16[32,1024]{1,0:T(8,128)(2,1)S(1)}, u32[]{:S(2)}, u32[]{:S(2)}) collective-permute-start(bf16[32,1024]{1,0:T(8,128)(2,1)S(1)} %dynamic-slice_bitcast_fusion.15), channel_id=1, source_target_pairs={{0,16},{1,17},{2,18},{3,19},{4,20},{5,21},{6,22},{7,23},{8,24},{9,... | collective-permute-start | bytes 196616 | tf_op jit(solution)/shard_map/ppermute | solution.py:156
  550.6 12.0 %collective-permute-start.13 = (f32[8,14336]{1,0:T(8,128)S(1)}, f32[8,14336]{1,0:T(8,128)S(1)}, u32[]{:S(2)}, u32[]{:S(2)}) collective-permute-start(f32[8,14336]{1,0:T(8,128)S(1)} %pad_maximum_fusion.3), channel_id=1, source_target_pairs={{0,8},{1,9},{2,10},{3,11},{4,12},{5,13},{6,14},{7,15},{8,0},{9,1},... | collective-permute-start | bytes 1376264 | tf_op jit(solution)/shard_map/ppermute | solution.py:156
  561.9 85.5 %collective-permute-start.35 = (bf16[2,2,2,2,128,1024]{5,4,0,1,2,3:T(8,128)(2,1)}, bf16[2,2,2,2,128,1024]{5,4,0,1,2,3:T(8,128)(2,1)}, u32[]{:S(2)}, u32[]{:S(2)}) collective-permute-start(bf16[2,2,2,2,128,1024]{5,4,0,1,2,3:T(8,128)(2,1)} %bitcast.239), channel_id=1, source_target_pairs={{0,2},{1,3},{2,0},{3,1},{4,6},{5,7},{6,4},{7,5},{8,10},{9,11},{10,... | collective-permute-start | bytes 12582920 | tf_op jit(solution)/shard_map/ppermute | solution.py:156
  562.8 43.3 %collective-permute-start.14 = (f32[16,14336]{1,0:T(8,128)S(1)}, f32[16,14336]{1,0:T(8,128)S(1)}, u32[]{:S(2)}, u32[]{:S(2)}) collective-permute-start(f32[16,14336]{1,0:T(8,128)S(1)} %pad_maximum_fusion.1), channel_id=1, source_target_pairs={{0,16},{1,17},{2,18},{3,19},{4,20},{5,21},{6,22},{7,23},{8,24},{9,... | collective-permute-start | bytes 2752520 | tf_op jit(solution)/shard_map/ppermute | solution.py:156
  615.5 3.7 collective-permute-start.15
  618.3 34.8 %collective-permute-start.20 = (bf16[2,2,2,2,32,3072]{5,4,0,3,2,1:T(8,128)(2,1)}, bf16[2,2,2,2,32,3072]{5,4,0,3,2,1:T(8,128)(2,1)S(1)}, u32[]{:S(2)}, u32[]{:S(2)}) collective-permute-start(bf16[2,2,2,2,32,3072]{5,4,0,3,2,1:T(8,128)(2,1)} %bitcast.241), channel_id=1, source_target_pairs={{0,2},{1,3},{2,0},{3,1},{4,6},{5,7},{6,4},{7,5},{8,10},{9,11},{10,... | collective-permute-start | bytes 9437192 | tf_op jit(solution)/shard_map/ppermute | solution.py:156
  619.2 4.8 collective-permute-start.16
  624.0 4.0 collective-permute-start.17
  628.0 4.3 collective-permute-start.18
  632.4 6.8 collective-permute-start.19
  645.2 44.6 %collective-permute-start.31 = (bf16[2,2,2,32,4096]{4,3,0,2,1:T(8,128)(2,1)S(1)}, bf16[2,2,2,32,4096]{4,3,0,2,1:T(8,128)(2,1)S(1)}, u32[]{:S(2)}, u32[]{:S(2)}) collective-permute-start(bf16[2,2,2,32,4096]{4,3,0,2,1:T(8,128)(2,1)S(1)} %dynamic-slice_bitcast_fusion.1), channel_id=1, source_target_pairs={{0,4},{1,5},{2,6},{3,7},{4,0},{5,1},{6,2},{7,3},{8,12},{9,13},{10,... | collective-permute-start | bytes 6291464 | tf_op jit(solution)/shard_map/ppermute | solution.py:156
  651.8 44.4 %collective-permute-start.36 = (bf16[2,2,2,128,1024]{4,3,0,1,2:T(8,128)(2,1)S(1)}, bf16[2,2,2,128,1024]{4,3,0,1,2:T(8,128)(2,1)S(1)}, u32[]{:S(2)}, u32[]{:S(2)}) collective-permute-start(bf16[2,2,2,128,1024]{4,3,0,1,2:T(8,128)(2,1)S(1)} %dynamic-slice_bitcast_fusion), channel_id=1, source_target_pairs={{0,1},{1,0},{2,3},{3,2},{4,5},{5,4},{6,7},{7,6},{8,9},{9,8},{10,11... | collective-permute-start | bytes 6291464 | tf_op jit(solution)/shard_map/ppermute | solution.py:156
  654.9 44.2 %collective-permute-start.21 = (bf16[2,2,2,32,3072]{4,3,0,2,1:T(8,128)(2,1)S(1)}, bf16[2,2,2,32,3072]{4,3,0,2,1:T(8,128)(2,1)S(1)}, u32[]{:S(2)}, u32[]{:S(2)}) collective-permute-start(bf16[2,2,2,32,3072]{4,3,0,2,1:T(8,128)(2,1)S(1)} %dynamic-slice_bitcast_fusion.2), channel_id=1, source_target_pairs={{0,8},{1,9},{2,10},{3,11},{4,12},{5,13},{6,14},{7,15},{8,0},{9,1},... | collective-permute-start | bytes 4718600 | tf_op jit(solution)/shard_map/ppermute | solution.py:156
  690.7 21.2 %collective-permute-start.32 = (bf16[2,2,32,4096]{3,2,0,1:T(8,128)(2,1)S(1)}, bf16[2,2,32,4096]{3,2,0,1:T(8,128)(2,1)S(1)}, u32[]{:S(2)}, u32[]{:S(2)}) collective-permute-start(bf16[2,2,32,4096]{3,2,0,1:T(8,128)(2,1)S(1)} %dynamic-slice_bitcast_fusion.4), channel_id=1, source_target_pairs={{0,8},{1,9},{2,10},{3,11},{4,12},{5,13},{6,14},{7,15},{8,0},{9,1},... | collective-permute-start | bytes 3145736 | tf_op jit(solution)/shard_map/ppermute | solution.py:156
  697.6 26.2 %collective-permute-start.37 = (bf16[2,2,128,1024]{3,2,0,1:T(8,128)(2,1)S(1)}, bf16[2,2,128,1024]{3,2,0,1:T(8,128)(2,1)S(1)}, u32[]{:S(2)}, u32[]{:S(2)}) collective-permute-start(bf16[2,2,128,1024]{3,2,0,1:T(8,128)(2,1)S(1)} %dynamic-slice_bitcast_fusion.3), channel_id=1, source_target_pairs={{0,4},{1,5},{2,6},{3,7},{4,0},{5,1},{6,2},{7,3},{8,12},{9,13},{10,... | collective-permute-start | bytes 3145736 | tf_op jit(solution)/shard_map/ppermute | solution.py:156
  699.7 35.7 %collective-permute-start.22 = (bf16[2,2,32,3072]{3,2,0,1:T(8,128)(2,1)S(1)}, bf16[2,2,32,3072]{3,2,0,1:T(8,128)(2,1)S(1)}, u32[]{:S(2)}, u32[]{:S(2)}) collective-permute-start(bf16[2,2,32,3072]{3,2,0,1:T(8,128)(2,1)S(1)} %dynamic-slice_bitcast_fusion.5), channel_id=1, source_target_pairs={{0,4},{1,5},{2,6},{3,7},{4,0},{5,1},{6,2},{7,3},{8,12},{9,13},{10,... | collective-permute-start | bytes 2359304 | tf_op jit(solution)/shard_map/ppermute | solution.py:156
  712.2 24.7 %collective-permute-start.33 = (bf16[2,32,4096]{2,1,0:T(8,128)(2,1)S(1)}, bf16[2,32,4096]{2,1,0:T(8,128)(2,1)S(1)}, u32[]{:S(2)}, u32[]{:S(2)}) collective-permute-start(bf16[2,32,4096]{2,1,0:T(8,128)(2,1)S(1)} %dynamic-slice_bitcast_fusion.7), channel_id=1, source_target_pairs={{0,1},{1,0},{2,3},{3,2},{4,5},{5,4},{6,7},{7,6},{8,9},{9,8},{10,11... | collective-permute-start | bytes 1572872 | tf_op jit(solution)/shard_map/ppermute | solution.py:156
  724.2 14.0 %collective-permute-start.38 = (bf16[2,128,1024]{2,1,0:T(8,128)(2,1)S(1)}, bf16[2,128,1024]{2,1,0:T(8,128)(2,1)S(1)}, u32[]{:S(2)}, u32[]{:S(2)}) collective-permute-start(bf16[2,128,1024]{2,1,0:T(8,128)(2,1)S(1)} %dynamic-slice_bitcast_fusion.6), channel_id=1, source_target_pairs={{0,8},{1,9},{2,10},{3,11},{4,12},{5,13},{6,14},{7,15},{8,0},{9,1},... | collective-permute-start | bytes 1572872 | tf_op jit(solution)/shard_map/ppermute | solution.py:156
  735.7 7.8 %collective-permute-start.23 = (bf16[2,32,3072]{2,1,0:T(8,128)(2,1)S(1)}, bf16[2,32,3072]{2,1,0:T(8,128)(2,1)S(1)}, u32[]{:S(2)}, u32[]{:S(2)}) collective-permute-start(bf16[2,32,3072]{2,1,0:T(8,128)(2,1)S(1)} %dynamic-slice_bitcast_fusion.9), channel_id=1, source_target_pairs={{0,1},{1,0},{2,3},{3,2},{4,5},{5,4},{6,7},{7,6},{8,9},{9,8},{10,11... | collective-permute-start | bytes 1179656 | tf_op jit(solution)/shard_map/ppermute | solution.py:156
  737.1 20.1 %collective-permute-start.34 = (bf16[32,4096]{1,0:T(8,128)(2,1)S(1)}, bf16[32,4096]{1,0:T(8,128)(2,1)S(1)}, u32[]{:S(2)}, u32[]{:S(2)}) collective-permute-start(bf16[32,4096]{1,0:T(8,128)(2,1)S(1)} %dynamic-slice_bitcast_fusion.11), channel_id=1, source_target_pairs={{0,16},{1,17},{2,18},{3,19},{4,20},{5,21},{6,22},{7,23},{8,24},{9,... | collective-permute-start | bytes 786440 | tf_op jit(solution)/shard_map/ppermute | solution.py:156
  738.4 24.4 %collective-permute-start.39 = (bf16[128,1024]{1,0:T(8,128)(2,1)S(1)}, bf16[128,1024]{1,0:T(8,128)(2,1)S(1)}, u32[]{:S(2)}, u32[]{:S(2)}) collective-permute-start(bf16[128,1024]{1,0:T(8,128)(2,1)S(1)} %dynamic-slice_bitcast_fusion.10), channel_id=1, source_target_pairs={{0,16},{1,17},{2,18},{3,19},{4,20},{5,21},{6,22},{7,23},{8,24},{9,... | collective-permute-start | bytes 786440 | tf_op jit(solution)/shard_map/ppermute | solution.py:156
  743.6 22.6 %collective-permute-start.24 = (bf16[32,3072]{1,0:T(8,128)(2,1)S(1)}, bf16[32,3072]{1,0:T(8,128)(2,1)S(1)}, u32[]{:S(2)}, u32[]{:S(2)}) collective-permute-start(bf16[32,3072]{1,0:T(8,128)(2,1)S(1)} %dynamic-slice_bitcast_fusion.13), channel_id=1, source_target_pairs={{0,16},{1,17},{2,18},{3,19},{4,20},{5,21},{6,22},{7,23},{8,24},{9,... | collective-permute-start | bytes 589832 | tf_op jit(solution)/shard_map/ppermute | solution.py:156
  (44 other events, 157.5 us)
Sparse Core Ops, SparseCore 0:
  10.9 74.4 all-gather.4
  88.5 57.9 all-gather.6
  149.6 82.9 all-gather.8
  235.6 77.9 all-gather.10

commit v2 on v1

--- a/solution.py
+++ b/solution.py
@@ -245,8 +245,10 @@
     cond_all = cond_all.reshape(dp_size * groups, -1).astype(jnp.float32)
     cond_columns = lax.dynamic_slice_in_dim(cond_all, flat_index() * own_cond, own_cond, 1)
     cond_columns = jax.nn.silu(cond_columns).astype(jnp.bfloat16)
-    proj_full = lax.all_gather(proj_weight, AXES, axis=0, tiled=True)
-    up_full = lax.all_gather(up_weight, AXES, axis=0, tiled=True)
+    proj_up = jnp.concatenate([proj_weight, up_weight], axis=1)
+    proj_up_full = lax.all_gather(proj_up, AXES, axis=0, tiled=True)
+    proj_full = proj_up_full[:, :model_width]
+    up_full = proj_up_full[:, model_width:]
     down_full = lax.all_gather(down_weight, AXES, axis=0, tiled=True)
     row_count = groups * local_len
     cond_float = cond_in.astype(jnp.float32)

time: 781 us -> 737 us (0.944)
  waiting for transfers between devices: 308 us -> 254 us
  blocking collectives: 55.5 us -> 69.2 us
    all_gather x1, waiting for transfers between devices: 62.1 us -> 15.5 us  [per_device(): down_full = lax.all_gather(down_weight, AXES, axis=0, tiled=True)]
    all_to_all x1, blocking collectives: 55.5 us -> 69.2 us  [per_device(): lax.all_to_all(mixed, 'seq', split_axis=3, concat_axis=2, tiled=True)]
    unnamed x134 -> x136, local copies, waits for them, and re-layouts: 31.8 us -> 30.6 us
  transfers between devices with their start and end apart: 47 -> 46, of which waited for: 34 -> 34; matrix products, arithmetic and copies ran while one was open for 26% -> 27% of each run, Pallas kernels for 8% -> 9%
where the time goes in v2:
time: 737 us; the launch traced here: 729 us
  waiting for transfers between devices  254 us (34%)
  local copies, waits for them, and re-layouts  107 us (15%)
  matrix products  98.3 us (13%)
  blocking collectives  69.2 us (9%)
  Pallas kernels  65.4 us (9%)
  other arithmetic  63.6 us (9%)
  starting transfers between devices  56.7 us (8%)
  between operations  15.2 us (2%)
    ppermute x40, waiting for transfers between devices, swap(): return lax.ppermute(values, AXES, pairs)  189 us
    all_to_all x1, blocking collectives, per_device(): lax.all_to_all(mixed, 'seq', split_axis=3, concat_axis=2, tiled=True)  69.2 us
    pallas_call x1, Pallas kernels, attend_back(): pl.pallas_call(functools.partial(attend_back_kernel, head_dim, min(length...  42.6 us
    ppermute x40, starting transfers between devices, swap(): return lax.ppermute(values, AXES, pairs)  41.2 us
    unnamed x136, local copies, waits for them, and re-layouts  30.6 us
    pallas_call x1, Pallas kernels, attend(): pl.pallas_call(functools.partial(attend_kernel, head_dim, min(length, 256...  22.8 us
    all_to_all x1, waiting for transfers between devices, per_device(): lax.all_to_all(grad_mixed, 'seq', split_axis=2, concat_axis=3, tiled=True)  20.6 us
    unnamed x3, other arithmetic  18.8 us
  transfers between devices with their start and end apart: 46, of which 34 were waited for; matrix products, arithmetic and copies ran while one was open for 27% of the time, Pallas kernels for 9%

profile of v2, /device:TPU:0, one launch (start us, length us, event | category | flops | bytes accessed | tf_op | source)
XLA Modules:
  0.0 729.5 jit_solution(11921902484567549233)
XLA Ops:
  10.5 3.4 concatenate.57
  13.9 3.0 collective-permute-start
  27.7 3.2 collective-permute-start.4
  36.8 12.1 %collective-permute-done.5 = f32[8,6144]{1,0:T(8,128)S(1)} collective-permute-done((f32[8,6144]{1,0:T(8,128)S(1)}, f32[8,6144]{1,0:T(8,128)S(1)}, u32[]{:S(2)}, u32[]{:S(2)}) %collective-permute-start.5) | collective-permute-done | bytes 196640 | tf_op jit(solution)/shard_map/ppermute | solution.py:156
  49.1 6.4 collective-permute-done.6
  56.9 2.9 collective-permute-done.7
  62.8 2.7 collective-permute-done.9
  66.2 18.6 %all-gather.4.cloned.1.call-done = bf16[1024,3072]{1,0:T(8,128)(2,1)} async-done(((bf16[32,3072]{1,0:T(8,128)(2,1)}), bf16[1024,3072]{1,0:T(8,128)(2,1)}) %all-gather.4.cloned.1.call-update) | async-done | bytes 6291472 | tf_op jit(solution)/shard_map/all_gather | solution.py:234
  84.9 7.9 %add_convert_fusion = bf16[512,3072]{1,0:T(8,128)(2,1)} fusion(bf16[1024,3072]{1,0:T(8,128)(2,1)} %all-gather.4.cloned.1.call-done, f32[3072]{0:T(1024)S(1)} %pad_maximum_fusion.14, bf16[1,512,1024]{2,1,0:T(8,128)(2,1)S(1)} %copy-done.5, f32[1024]{0:T(1024)S(1)} %bitcast.288, f32[1024]{0:T(1024)S(1)} %bitcast.264, f32[512]{0:T(512)S(1)} %add_rsqrt_fusion.1, ...), kind=kOutput, calls=%fused_computation.24 | convolution fusion | flops 3227516928 | bytes 10510336 | tf_op jit(solution)/shard_map/dot_general | solution.py:272
  92.7 3.2 copy.83
  95.9 2.7 copy.84
  98.7 69.2 %all_to_all.69 = bf16[1,3,512,1024]{2,1,0,3:T(4,128)(2,1)S(1)} all-to-all(bf16[1,3,512,1024]{2,1,0,3:T(4,128)(2,1)S(1)} %copy.84), channel_id=1, replica_groups=mesh['dp'=16,'seq'=2] {'seq'}, dimensions={3} | all-to-all | bytes 6291456 | tf_op jit(solution)/shard_map/all_to_all | solution.py:275
  170.3 3.3 copy.86
  173.5 22.8 %shard_map.228 = bf16[1,1024,512]{2,1,0:T(8,128)(2,1)S(1)} custom-call(bf16[1,3,1024,512]{3,2,1,0:T(8,128)(2,1)S(1)} %bitcast.241), custom_call_target="tpu_custom_call" | custom-call | flops 8589934592 | bytes 4194304 | tf_op jit(solution)/shard_map/pallas_call | solution.py:106
  196.4 2.9 copy.131
  199.9 9.0 %reduce.33 = bf16[1024,512]{1,0:T(8,128)(2,1)} reduce(bf16[1024,1,512]{2,1,0:T(2,128)(2,1)} %bitcast.253, bf16[]{:T(256)} %broadcast.173), dimensions={1}, to_apply=%bitcast.239.reduce_sub_computation | reduce | bytes 2097154
  208.9 2.6 reshape.362
  211.5 4.4 all-to-all-start.1
  222.9 9.2 %all-to-all-done.1 = bf16[2,2,131072]{2,1,0:T(2,128)(2,1)} async-done(((bf16[2,2,131072]{2,1,0:T(2,128)(2,1)}), bf16[2,2,131072]{2,1,0:T(2,128)(2,1)}, u32[]{:S(2)}, u32[]{:S(2)}) %all-to-all-start.1) | async-done | bytes 1048608 | tf_op jit(solution)/shard_map/all_to_all | solution.py:278
  232.1 3.1 reshape.363
  235.2 2.8 copy.103
  240.4 5.0 fusion.93
  246.7 7.0 fusion.11
  253.7 15.5 %all-gather.8.cloned.1.call-done = bf16[4096,1024]{1,0:T(8,128)(2,1)} async-done(((bf16[128,1024]{1,0:T(8,128)(2,1)}), bf16[4096,1024]{1,0:T(8,128)(2,1)}) %all-gather.8.cloned.1.call-update) | async-done | bytes 8388624 | tf_op jit(solution)/shard_map/all_gather | solution.py:252
  269.2 16.6 %convert_reduce_fusion = (f32[4096]{0:T(1024)}, bf16[512,4096]{1,0:T(8,128)(2,1)}) fusion(f32[512,4096]{1,0:T(8,128)} %fusion.11, f32[4096]{0:T(1024)} %bitcast_convert_fusion, bf16[4096,1024]{1,0:T(8,128)(2,1)} %all-gather.8.cloned.1.call-done, bf16[1,512,1024]{2,1,0:T(8,128)(2,1)} %param.25, f32[1024]{0:T(1024)S(1)} %bitcast.277), kind=kOutput, calls=%fused_computation.13 | convolution fusion | flops 4344770560 | bytes 22056960 | tf_op jit(solution)/shard_map/dot_general | solution.py:303
  285.9 9.4 %fusion.36 = (f32[1024]{0:T(1024)}, f32[512]{0:T(512)S(1)}, f32[512,1024]{1,0:T(8,128)S(1)}) fusion(f32[1,512,1024]{2,1,0:T(8,128)S(1)} %copy-done.19, f32[512]{0:T(512)S(1)} %copy-done.57, f32[512]{0:T(512)S(1)} %broadcast_multiply_fusion.4, f32[1024]{0:T(1024)S(1)} %bitcast.272, bf16[512,4096]{1,0:T(8,128)(2,1)} %get-tuple-element.89, ...), kind=kOutput, calls=%fused_computation.67 | convolution fusion | flops 4298635776 | bytes 16791552 | tf_op jit(solution)/shard_map/dot_general | solution.py:308
  295.6 10.8 %fusion.32 = (f32[1024]{0:T(1024)}, bf16[1,512,1024]{2,1,0:T(8,128)(2,1)}, f32[1024]{0:T(1024)}, f32[1,512,1024]{2,1,0:T(8,128)S(1)}) fusion(bf16[1,512,1024]{2,1,0:T(8,128)(2,1)S(1)} %copy-done.25, f32[1024]{0:T(1024)S(1)} %copy-done.52, f32[1,512,1024]{2,1,0:T(8,128)S(1)} %copy-done.19, f32[1024]{0:T(1024)S(1)} %bitcast.278, ...), kind=kOutput, calls=%fused_computation.59 | convolution fusion | flops 4325373952 | bytes 27312128 | tf_op jit(solution)/shard_map/dot_general | solution.py:292
  309.6 3.9 fusion.49
  313.5 6.0 copy.89
  319.4 9.0 %reduce.34 = bf16[1024,512]{1,0:T(8,128)(2,1)} reduce(bf16[1024,1,512]{2,1,0:T(2,128)(2,1)} %bitcast.254, bf16[]{:T(256)} %broadcast.173), dimensions={1}, to_apply=%bitcast.211.reduce_sub_computation | reduce | bytes 2097154
  328.5 2.6 reshape.364
  331.1 4.9 all-to-all-start.2
  336.0 13.9 %convolution_convert_fusion = bf16[4096,1024]{1,0:T(8,128)(2,1)} fusion(bf16[1,512,1024]{2,1,0:T(8,128)(2,1)} %param.25, f32[1024]{0:T(1024)S(1)} %bitcast.279, f32[512,4096]{1,0:T(8,128)} %fusion.11, f32[4096]{0:T(1024)} %bitcast_convert_fusion), kind=kOutput, calls=%fused_computation.15 | convolution fusion | flops 4321705984 | bytes 17846272 | tf_op jit(solution)/shard_map/dot_general | solution.py:300
  353.7 3.1 reshape.365
  356.8 2.9 copy.104
  363.2 42.6 %shard_map.229 = bf16[1,3,1024,512]{3,2,1,0:T(8,128)(2,1)S(1)} custom-call(bf16[1,3,1024,512]{3,2,1,0:T(8,128)(2,1)S(1)} %bitcast.242, bf16[1,1024,512]{2,1,0:T(8,128)(2,1)S(1)} %bitcast.243), custom_call_target="tpu_custom_call" | custom-call | flops 21474836480 | bytes 7340032 | tf_op jit(solution)/shard_map/pallas_call | solution.py:122
  405.8 4.7 copy.91
  410.5 6.0 all-to-all-start.3
  416.5 7.6 %convolution_convert_fusion.1 = bf16[1024,4096]{1,0:T(8,128)(2,1)S(1)} fusion(bf16[512,4096]{1,0:T(8,128)(2,1)} %get-tuple-element.89, f32[1,512,1024]{2,1,0:T(8,128)} %copy-done.18, f32[1024]{0:T(1024)S(1)} %bitcast.291, f32[1024]{0:T(1024)S(1)} %bitcast.275, f32[512]{0:T(512)S(1)} %copy-done.58, f32[512]{0:T(512)S(1)} %copy-done.43), kind=kOutput, calls=%fused_computation.16 | convolution fusion | flops 4301783040 | bytes 14692352 | tf_op jit(solution)/shard_map/dot_general | solution.py:305
  428.2 2.8 constant_dynamic-slice_fusion.3
  433.4 7.6 %collective-permute-done.26 = bf16[2,2,2,32,1024]{4,3,0,2,1:T(8,128)(2,1)S(1)} collective-permute-done((bf16[2,2,2,32,1024]{4,3,0,2,1:T(8,128)(2,1)}, bf16[2,2,2,32,1024]{4,3,0,2,1:T(8,128)(2,1)S(1)}, u32[]{:S(2)}, u32[]{:S(2)}) %collective-permute-start.26) | collective-permute-done | bytes 524320 | tf_op jit(solution)/shard_map/ppermute | solution.py:156
  444.1 20.6 %all-to-all-done.3 = bf16[1,3,1024,512]{3,1,0,2:T(4,128)(2,1)} async-done(((bf16[1,3,1024,512]{3,1,0,2:T(4,128)(2,1)}), bf16[1,3,1024,512]{3,1,0,2:T(4,128)(2,1)}, u32[]{:S(2)}, u32[]{:S(2)}) %all-to-all-start.3) | async-done | bytes 3145760 | tf_op jit(solution)/shard_map/all_to_all | solution.py:323
  464.8 3.0 copy.92
  467.8 3.2 copy.93
  473.8 7.7 %fusion.29 = (f32[1024]{0:T(1024)}, f32[512]{0:T(512)}, f32[512,1024]{1,0:T(8,128)S(1)}) fusion(bf16[1,512,1024]{2,1,0:T(8,128)(2,1)} %param.13, f32[512]{0:T(512)S(1)} %copy-done.45, f32[512]{0:T(512)S(1)} %copy-done.32, f32[1024]{0:T(1024)S(1)} %bitcast.265, bf16[512,3072]{0,1:T(8,128)(2,1)S(1)} %bitcast.247, ...), kind=kOutput, calls=%fused_computation.56 | convolution fusion | flops 3225418240 | bytes 12597248 | tf_op jit(solution)/shard_map/dot_general | solution.py:329
  492.7 3.2 collective-permute-done.10
  500.0 2.9 collective-permute-done.28
  508.1 6.9 constant_dynamic-slice_fusion.1
  515.0 2.7 copy.127
  520.5 4.4 convolution_convert_fusion.2
  527.9 34.0 %collective-permute-done.14 = f32[16,14336]{1,0:T(8,128)S(1)} collective-permute-done((f32[16,14336]{1,0:T(8,128)S(1)}, f32[16,14336]{1,0:T(8,128)S(1)}, u32[]{:S(2)}, u32[]{:S(2)}) %collective-permute-start.14) | collective-permute-done | bytes 917536 | tf_op jit(solution)/shard_map/ppermute | solution.py:156
  567.0 2.8 reduce_sum.207
  584.0 4.1 collective-permute-done.18
  592.4 2.6 collective-permute-done.19
  595.8 5.0 fusion.8
  603.1 4.3 fusion.7
  610.7 34.8 %collective-permute-done.31 = bf16[2,2,2,32,4096]{4,3,0,2,1:T(8,128)(2,1)S(1)} collective-permute-done((bf16[2,2,2,32,4096]{4,3,0,2,1:T(8,128)(2,1)S(1)}, bf16[2,2,2,32,4096]{4,3,0,2,1:T(8,128)(2,1)S(1)}, u32[]{:S(2)}, u32[]{:S(2)}) %collective-permute-start.31) | collective-permute-done | bytes 2097184 | tf_op jit(solution)/shard_map/ppermute | solution.py:156
  646.6 5.5 collective-permute-done.36
  656.2 11.5 %collective-permute-done.32 = bf16[2,2,32,4096]{3,2,0,1:T(8,128)(2,1)S(1)} collective-permute-done((bf16[2,2,32,4096]{3,2,0,1:T(8,128)(2,1)S(1)}, bf16[2,2,32,4096]{3,2,0,1:T(8,128)(2,1)S(1)}, u32[]{:S(2)}, u32[]{:S(2)}) %collective-permute-start.32) | collective-permute-done | bytes 1048608 | tf_op jit(solution)/shard_map/ppermute | solution.py:156
  669.2 10.3 %collective-permute-done.37 = bf16[2,2,128,1024]{3,2,0,1:T(8,128)(2,1)S(1)} collective-permute-done((bf16[2,2,128,1024]{3,2,0,1:T(8,128)(2,1)S(1)}, bf16[2,2,128,1024]{3,2,0,1:T(8,128)(2,1)S(1)}, u32[]{:S(2)}, u32[]{:S(2)}) %collective-permute-start.37) | collective-permute-done | bytes 1048608 | tf_op jit(solution)/shard_map/ppermute | solution.py:156
  680.0 11.1 %collective-permute-done.22 = bf16[2,2,32,3072]{3,2,0,1:T(8,128)(2,1)S(1)} collective-permute-done((bf16[2,2,32,3072]{3,2,0,1:T(8,128)(2,1)S(1)}, bf16[2,2,32,3072]{3,2,0,1:T(8,128)(2,1)S(1)}, u32[]{:S(2)}, u32[]{:S(2)}) %collective-permute-start.22) | collective-permute-done | bytes 786464 | tf_op jit(solution)/shard_map/ppermute | solution.py:156
  696.1 3.1 collective-permute-done.23
  700.5 12.4 %collective-permute-done.34 = bf16[32,4096]{1,0:T(8,128)(2,1)S(1)} collective-permute-done((bf16[32,4096]{1,0:T(8,128)(2,1)S(1)}, bf16[32,4096]{1,0:T(8,128)(2,1)S(1)}, u32[]{:S(2)}, u32[]{:S(2)}) %collective-permute-start.34) | collective-permute-done | bytes 262176 | tf_op jit(solution)/shard_map/ppermute | solution.py:156
  713.8 4.8 collective-permute-done.39
  (334 shorter events, 136.0 us)
Async XLA Ops:
  7.2 26.9 %copy-start = (bf16[32,6144]{1,0:T(8,128)(2,1)S(1)}, bf16[32,6144]{1,0:T(8,128)(2,1)}, u32[]{:S(2)}) copy-start(bf16[32,6144]{1,0:T(8,128)(2,1)} %param.15) | copy-start | bytes 1179652
  7.2 23.7 %copy-start.5 = (bf16[1,512,1024]{2,1,0:T(8,128)(2,1)S(1)}, bf16[1,512,1024]{2,1,0:T(8,128)(2,1)}, u32[]{:S(2)}) copy-start(bf16[1,512,1024]{2,1,0:T(8,128)(2,1)} %param.13) | copy-start | bytes 3145732
  7.2 77.6 %all-gather.4.cloned.1.call-start = ((), (), s32[]{:S(2)}) async-start(), calls=%async_computation.4 | async-start | bytes 6488064 | tf_op jit(solution)/shard_map/all_gather | solution.py:234
  7.9 232.4 %all-gather.6.cloned.1.call-start = ((), (), s32[]{:S(2)}) async-start(), calls=%async_computation.5 | async-start | bytes 10813440 | tf_op jit(solution)/shard_map/all_gather | solution.py:249
  9.7 259.5 %all-gather.8.cloned.1.call-start = ((), (), s32[]{:S(2)}) async-start(), calls=%async_computation.6 | async-start | bytes 8650752 | tf_op jit(solution)/shard_map/all_gather | solution.py:252
  13.9 4.6 collective-permute-start
  18.6 1.2 collective-permute-start.1
  19.9 3.8 collective-permute-start.2
  23.7 3.9 collective-permute-start.3
  25.8 59.0 %copy-start.31 = (f32[512]{0:T(512)}, f32[512]{0:T(512)S(1)}, u32[]{:S(2)}) copy-start(f32[512]{0:T(512)S(1)} %broadcast_multiply_fusion.5) | copy-start | bytes 6148
  27.7 6.1 collective-permute-start.4
  33.8 51.0 %copy-start.21 = (bf16[16,1472]{1,0:T(8,128)(2,1)}, bf16[16,1472]{1,0:T(8,128)(2,1)S(1)}, u32[]{:S(2)}) copy-start(bf16[16,1472]{1,0:T(8,128)(2,1)S(1)} %get-tuple-element.57) | copy-start | bytes 141316
  33.9 51.0 %copy-start.22 = (bf16[16,1472]{1,0:T(8,128)(2,1)}, bf16[16,1472]{1,0:T(8,128)(2,1)S(1)}, u32[]{:S(2)}) copy-start(bf16[16,1472]{1,0:T(8,128)(2,1)S(1)} %get-tuple-element.58) | copy-start | bytes 141316
  34.1 22.8 %copy-start.27 = (f32[16,1,1,32]{3,1,0,2:T(1,128)}, f32[16,1,1,32]{3,1,0,2:T(1,128)S(1)}, u32[]{:S(2)}) copy-start(f32[16,1,1,32]{3,1,0,2:T(1,128)S(1)} %fusion.78) | copy-start | bytes 6148
  34.3 14.5 %collective-permute-start.5 = (f32[8,6144]{1,0:T(8,128)S(1)}, f32[8,6144]{1,0:T(8,128)S(1)}, u32[]{:S(2)}, u32[]{:S(2)}) collective-permute-start(f32[8,6144]{1,0:T(8,128)S(1)} %constant_dynamic-slice_fusion.11), channel_id=1, source_target_pairs={{0,16},{1,17},{2,18},{3,19},{4,20},{5,21},{6,22},{7,23},{8,24},{9,... | collective-permute-start | bytes 589832 | tf_op jit(solution)/shard_map/ppermute | solution.py:156
  36.8 48.0 %copy-start.44 = (f32[512]{0:T(512)}, f32[512]{0:T(512)S(1)}, u32[]{:S(2)}) copy-start(f32[512]{0:T(512)S(1)} %add_rsqrt_fusion.1) | copy-start | bytes 6148
  48.9 6.5 collective-permute-start.6
  55.5 4.2 collective-permute-start.7
  59.8 1.3 collective-permute-start.8
  61.1 4.4 collective-permute-start.9
  66.2 18.6 %copy-start.29 = (f32[1,1,1,1024]{3,1,2,0:T(1,128)}, f32[1,1,1,1024]{3,1,2,0:T(1,128)S(1)}, u32[]{:S(2)}) copy-start(f32[1,1,1,1024]{3,1,2,0:T(1,128)S(1)} %get-tuple-element.71) | copy-start | bytes 12292
  66.2 18.6 %copy-start.48 = (f32[1,1,1,1024]{3,1,2,0:T(1,128)}, f32[1,1,1,1024]{3,1,2,0:T(1,128)S(1)}, u32[]{:S(2)}) copy-start(f32[1,1,1,1024]{3,1,2,0:T(1,128)S(1)} %get-tuple-element.70) | copy-start | bytes 12292
  211.5 20.6 %all-to-all-start.1 = ((bf16[2,2,131072]{2,1,0:T(2,128)(2,1)}), bf16[2,2,131072]{2,1,0:T(2,128)(2,1)}, u32[]{:S(2)}, u32[]{:S(2)}) async-start(bf16[2,2,131072]{2,1,0:T(2,128)(2,1)} %reshape.362), calls=%async_computation.1 | async-start | bytes 2097152 | tf_op jit(solution)/shard_map/all_to_all | solution.py:278
  245.4 40.4 %copy-start.42 = (f32[512]{0:T(512)}, f32[512]{0:T(512)S(1)}, u32[]{:S(2)}) copy-start(f32[512]{0:T(512)S(1)} %broadcast_multiply_fusion.4) | copy-start | bytes 6148
  246.7 22.5 %copy-start.34 = (f32[1,1,1,1024]{3,1,2,0:T(1,128)S(1)}, f32[1,1,1,1024]{3,1,2,0:T(1,128)}, u32[]{:S(2)}) copy-start(f32[1,1,1,1024]{3,1,2,0:T(1,128)} %get-tuple-element.67) | copy-start | bytes 12292
  269.2 16.6 %copy-start.19 = (f32[1,512,1024]{2,1,0:T(8,128)S(1)}, f32[1,512,1024]{2,1,0:T(8,128)}, u32[]{:S(2)}) copy-start(f32[1,512,1024]{2,1,0:T(8,128)} %copy-done.18) | copy-start | bytes 6291460
  269.2 16.6 %copy-start.57 = (f32[512]{0:T(512)S(1)}, f32[512]{0:T(512)}, u32[]{:S(2)}) copy-start(f32[512]{0:T(512)} %copy-done.56) | copy-start | bytes 6148
  331.1 22.6 %all-to-all-start.2 = ((bf16[2,2,131072]{2,1,0:T(2,128)(2,1)}), bf16[2,2,131072]{2,1,0:T(2,128)(2,1)}, u32[]{:S(2)}, u32[]{:S(2)}) async-start(bf16[2,2,131072]{2,1,0:T(2,128)(2,1)} %reshape.364), calls=%async_computation.2 | async-start | bytes 2097152 | tf_op jit(solution)/shard_map/all_to_all | solution.py:321
  336.0 13.9 %copy-start.24 = (bf16[512,1024]{1,0:T(8,128)(2,1)S(1)}, bf16[512,1024]{1,0:T(8,128)(2,1)}, u32[]{:S(2)}) copy-start(bf16[512,1024]{1,0:T(8,128)(2,1)} %copy-done.23) | copy-start | bytes 3145732
  336.0 13.9 %copy-start.26 = (bf16[1,512,2,512]{1,3,2,0:T(8,128)(2,1)S(1)}, bf16[1,512,2,512]{1,3,2,0:T(8,128)(2,1)}, u32[]{:S(2)}) copy-start(bf16[1,512,2,512]{1,3,2,0:T(8,128)(2,1)} %copy.88) | copy-start | bytes 3145732
  353.5 70.7 %collective-permute-start.25 = (bf16[2,2,2,2,32,1024]{5,4,0,3,2,1:T(8,128)(2,1)}, bf16[2,2,2,2,32,1024]{5,4,0,3,2,1:T(8,128)(2,1)}, u32[]{:S(2)}, u32[]{:S(2)}) collective-permute-start(bf16[2,2,2,2,32,1024]{5,4,0,3,2,1:T(8,128)(2,1)} %bitcast.238), channel_id=1, source_target_pairs={{0,2},{1,3},{2,0},{3,1},{4,6},{5,7},{6,4},{7,5},{8,10},{9,11},{10,... | collective-permute-start | bytes 3145736 | tf_op jit(solution)/shard_map/ppermute | solution.py:156
  410.5 54.3 %all-to-all-start.3 = ((bf16[1,3,1024,512]{3,1,0,2:T(4,128)(2,1)}), bf16[1,3,1024,512]{3,1,0,2:T(4,128)(2,1)}, u32[]{:S(2)}, u32[]{:S(2)}) async-start(bf16[1,3,1024,512]{3,1,0,2:T(4,128)(2,1)} %copy.91), calls=%async_computation.3 | async-start | bytes 8388608 | tf_op jit(solution)/shard_map/all_to_all | solution.py:323
  426.7 14.3 %collective-permute-start.26 = (bf16[2,2,2,32,1024]{4,3,0,2,1:T(8,128)(2,1)}, bf16[2,2,2,32,1024]{4,3,0,2,1:T(8,128)(2,1)S(1)}, u32[]{:S(2)}, u32[]{:S(2)}) collective-permute-start(bf16[2,2,2,32,1024]{4,3,0,2,1:T(8,128)(2,1)} %dynamic-slice_bitcast_fusion.8), channel_id=1, source_target_pairs={{0,8},{1,9},{2,10},{3,11},{4,12},{5,13},{6,14},{7,15},{8,0},{9,1},... | collective-permute-start | bytes 1572872 | tf_op jit(solution)/shard_map/ppermute | solution.py:156
  433.4 162.4 %collective-permute-start.30 = (bf16[2,2,2,2,32,4096]{5,4,0,3,1,2:T(8,128)(2,1)}, bf16[2,2,2,2,32,4096]{5,4,0,3,1,2:T(8,128)(2,1)}, u32[]{:S(2)}, u32[]{:S(2)}) collective-permute-start(bf16[2,2,2,2,32,4096]{5,4,0,3,1,2:T(8,128)(2,1)} %bitcast.236), channel_id=1, source_target_pairs={{0,2},{1,3},{2,0},{3,1},{4,6},{5,7},{6,4},{7,5},{8,10},{9,11},{10,... | collective-permute-start | bytes 12582920 | tf_op jit(solution)/shard_map/ppermute | solution.py:156
  442.7 48.8 %collective-permute-start.27 = (bf16[2,2,32,1024]{3,2,0,1:T(8,128)(2,1)}, bf16[2,2,32,1024]{3,2,0,1:T(8,128)(2,1)}, u32[]{:S(2)}, u32[]{:S(2)}) collective-permute-start(bf16[2,2,32,1024]{3,2,0,1:T(8,128)(2,1)} %dynamic-slice_bitcast_fusion.12), channel_id=1, source_target_pairs={{0,4},{1,5},{2,6},{3,7},{4,0},{5,1},{6,2},{7,3},{8,12},{9,13},{10,... | collective-permute-start | bytes 786440 | tf_op jit(solution)/shard_map/ppermute | solution.py:156
  473.8 11.1 %copy-start.36 = (f32[1024]{0:T(1024)S(1)}, f32[1024]{0:T(1024)}, u32[]{:S(2)}) copy-start(f32[1024]{0:T(1024)} %get-tuple-element.25) | copy-start | bytes 12292
  473.8 11.7 %copy-start.40 = (f32[4096]{0:T(1024)S(1)}, f32[4096]{0:T(1024)}, u32[]{:S(2)}) copy-start(f32[4096]{0:T(1024)} %get-tuple-element.88) | copy-start | bytes 49156
  491.5 4.4 collective-permute-start.10
  496.9 1.4 collective-permute-start.11
  497.0 6.0 collective-permute-start.28
  498.5 7.7 %collective-permute-start.12 = (f32[4,14336]{1,0:T(4,128)S(1)}, f32[4,14336]{1,0:T(4,128)S(1)}, u32[]{:S(2)}, u32[]{:S(2)}) collective-permute-start(f32[4,14336]{1,0:T(4,128)S(1)} %pad_maximum_fusion.5), channel_id=1, source_target_pairs={{0,4},{1,5},{2,6},{3,7},{4,0},{5,1},{6,2},{7,3},{8,12},{9,13},{10,... | collective-permute-start | bytes 688136 | tf_op jit(solution)/shard_map/ppermute | solution.py:156
  503.0 14.8 %collective-permute-start.29 = (bf16[32,1024]{1,0:T(8,128)(2,1)S(1)}, bf16[32,1024]{1,0:T(8,128)(2,1)S(1)}, u32[]{:S(2)}, u32[]{:S(2)}) collective-permute-start(bf16[32,1024]{1,0:T(8,128)(2,1)S(1)} %dynamic-slice_bitcast_fusion.15), channel_id=1, source_target_pairs={{0,16},{1,17},{2,18},{3,19},{4,20},{5,21},{6,22},{7,23},{8,24},{9,... | collective-permute-start | bytes 196616 | tf_op jit(solution)/shard_map/ppermute | solution.py:156
  506.5 11.9 %collective-permute-start.13 = (f32[8,14336]{1,0:T(8,128)S(1)}, f32[8,14336]{1,0:T(8,128)S(1)}, u32[]{:S(2)}, u32[]{:S(2)}) collective-permute-start(f32[8,14336]{1,0:T(8,128)S(1)} %pad_maximum_fusion.3), channel_id=1, source_target_pairs={{0,8},{1,9},{2,10},{3,11},{4,12},{5,13},{6,14},{7,15},{8,0},{9,1},... | collective-permute-start | bytes 1376264 | tf_op jit(solution)/shard_map/ppermute | solution.py:156
  517.7 85.4 %collective-permute-start.35 = (bf16[2,2,2,2,128,1024]{5,4,0,1,2,3:T(8,128)(2,1)}, bf16[2,2,2,2,128,1024]{5,4,0,1,2,3:T(8,128)(2,1)}, u32[]{:S(2)}, u32[]{:S(2)}) collective-permute-start(bf16[2,2,2,2,128,1024]{5,4,0,1,2,3:T(8,128)(2,1)} %bitcast.235), channel_id=1, source_target_pairs={{0,2},{1,3},{2,0},{3,1},{4,6},{5,7},{6,4},{7,5},{8,10},{9,11},{10,... | collective-permute-start | bytes 12582920 | tf_op jit(solution)/shard_map/ppermute | solution.py:156
  518.6 43.3 %collective-permute-start.14 = (f32[16,14336]{1,0:T(8,128)S(1)}, f32[16,14336]{1,0:T(8,128)S(1)}, u32[]{:S(2)}, u32[]{:S(2)}) collective-permute-start(f32[16,14336]{1,0:T(8,128)S(1)} %pad_maximum_fusion.1), channel_id=1, source_target_pairs={{0,16},{1,17},{2,18},{3,19},{4,20},{5,21},{6,22},{7,23},{8,24},{9,... | collective-permute-start | bytes 2752520 | tf_op jit(solution)/shard_map/ppermute | solution.py:156
  562.1 10.1 %copy-start.41 = (f32[512]{0:T(512)S(1)}, f32[512]{0:T(512)}, u32[]{:S(2)}) copy-start(f32[512]{0:T(512)} %get-tuple-element.20) | copy-start | bytes 6148
  571.3 3.7 collective-permute-start.15
  574.1 34.8 %collective-permute-start.20 = (bf16[2,2,2,2,32,3072]{5,4,0,3,2,1:T(8,128)(2,1)}, bf16[2,2,2,2,32,3072]{5,4,0,3,2,1:T(8,128)(2,1)S(1)}, u32[]{:S(2)}, u32[]{:S(2)}) collective-permute-start(bf16[2,2,2,2,32,3072]{5,4,0,3,2,1:T(8,128)(2,1)} %bitcast.237), channel_id=1, source_target_pairs={{0,2},{1,3},{2,0},{3,1},{4,6},{5,7},{6,4},{7,5},{8,10},{9,11},{10,... | collective-permute-start | bytes 9437192 | tf_op jit(solution)/shard_map/ppermute | solution.py:156
  575.0 4.8 collective-permute-start.16
  579.8 4.0 collective-permute-start.17
  583.8 4.3 collective-permute-start.18
  588.2 6.8 collective-permute-start.19
  601.0 44.6 %collective-permute-start.31 = (bf16[2,2,2,32,4096]{4,3,0,2,1:T(8,128)(2,1)S(1)}, bf16[2,2,2,32,4096]{4,3,0,2,1:T(8,128)(2,1)S(1)}, u32[]{:S(2)}, u32[]{:S(2)}) collective-permute-start(bf16[2,2,2,32,4096]{4,3,0,2,1:T(8,128)(2,1)S(1)} %dynamic-slice_bitcast_fusion.1), channel_id=1, source_target_pairs={{0,4},{1,5},{2,6},{3,7},{4,0},{5,1},{6,2},{7,3},{8,12},{9,13},{10,... | collective-permute-start | bytes 6291464 | tf_op jit(solution)/shard_map/ppermute | solution.py:156
  607.6 44.4 %collective-permute-start.36 = (bf16[2,2,2,128,1024]{4,3,0,1,2:T(8,128)(2,1)S(1)}, bf16[2,2,2,128,1024]{4,3,0,1,2:T(8,128)(2,1)S(1)}, u32[]{:S(2)}, u32[]{:S(2)}) collective-permute-start(bf16[2,2,2,128,1024]{4,3,0,1,2:T(8,128)(2,1)S(1)} %dynamic-slice_bitcast_fusion), channel_id=1, source_target_pairs={{0,1},{1,0},{2,3},{3,2},{4,5},{5,4},{6,7},{7,6},{8,9},{9,8},{10,11... | collective-permute-start | bytes 6291464 | tf_op jit(solution)/shard_map/ppermute | solution.py:156
  610.7 44.2 %collective-permute-start.21 = (bf16[2,2,2,32,3072]{4,3,0,2,1:T(8,128)(2,1)S(1)}, bf16[2,2,2,32,3072]{4,3,0,2,1:T(8,128)(2,1)S(1)}, u32[]{:S(2)}, u32[]{:S(2)}) collective-permute-start(bf16[2,2,2,32,3072]{4,3,0,2,1:T(8,128)(2,1)S(1)} %dynamic-slice_bitcast_fusion.2), channel_id=1, source_target_pairs={{0,8},{1,9},{2,10},{3,11},{4,12},{5,13},{6,14},{7,15},{8,0},{9,1},... | collective-permute-start | bytes 4718600 | tf_op jit(solution)/shard_map/ppermute | solution.py:156
  646.5 21.2 %collective-permute-start.32 = (bf16[2,2,32,4096]{3,2,0,1:T(8,128)(2,1)S(1)}, bf16[2,2,32,4096]{3,2,0,1:T(8,128)(2,1)S(1)}, u32[]{:S(2)}, u32[]{:S(2)}) collective-permute-start(bf16[2,2,32,4096]{3,2,0,1:T(8,128)(2,1)S(1)} %dynamic-slice_bitcast_fusion.4), channel_id=1, source_target_pairs={{0,8},{1,9},{2,10},{3,11},{4,12},{5,13},{6,14},{7,15},{8,0},{9,1},... | collective-permute-start | bytes 3145736 | tf_op jit(solution)/shard_map/ppermute | solution.py:156
  653.3 26.2 %collective-permute-start.37 = (bf16[2,2,128,1024]{3,2,0,1:T(8,128)(2,1)S(1)}, bf16[2,2,128,1024]{3,2,0,1:T(8,128)(2,1)S(1)}, u32[]{:S(2)}, u32[]{:S(2)}) collective-permute-start(bf16[2,2,128,1024]{3,2,0,1:T(8,128)(2,1)S(1)} %dynamic-slice_bitcast_fusion.3), channel_id=1, source_target_pairs={{0,4},{1,5},{2,6},{3,7},{4,0},{5,1},{6,2},{7,3},{8,12},{9,13},{10,... | collective-permute-start | bytes 3145736 | tf_op jit(solution)/shard_map/ppermute | solution.py:156
  655.5 35.7 %collective-permute-start.22 = (bf16[2,2,32,3072]{3,2,0,1:T(8,128)(2,1)S(1)}, bf16[2,2,32,3072]{3,2,0,1:T(8,128)(2,1)S(1)}, u32[]{:S(2)}, u32[]{:S(2)}) collective-permute-start(bf16[2,2,32,3072]{3,2,0,1:T(8,128)(2,1)S(1)} %dynamic-slice_bitcast_fusion.5), channel_id=1, source_target_pairs={{0,4},{1,5},{2,6},{3,7},{4,0},{5,1},{6,2},{7,3},{8,12},{9,13},{10,... | collective-permute-start | bytes 2359304 | tf_op jit(solution)/shard_map/ppermute | solution.py:156
  668.0 24.7 %collective-permute-start.33 = (bf16[2,32,4096]{2,1,0:T(8,128)(2,1)S(1)}, bf16[2,32,4096]{2,1,0:T(8,128)(2,1)S(1)}, u32[]{:S(2)}, u32[]{:S(2)}) collective-permute-start(bf16[2,32,4096]{2,1,0:T(8,128)(2,1)S(1)} %dynamic-slice_bitcast_fusion.7), channel_id=1, source_target_pairs={{0,1},{1,0},{2,3},{3,2},{4,5},{5,4},{6,7},{7,6},{8,9},{9,8},{10,11... | collective-permute-start | bytes 1572872 | tf_op jit(solution)/shard_map/ppermute | solution.py:156
  680.0 14.0 %collective-permute-start.38 = (bf16[2,128,1024]{2,1,0:T(8,128)(2,1)S(1)}, bf16[2,128,1024]{2,1,0:T(8,128)(2,1)S(1)}, u32[]{:S(2)}, u32[]{:S(2)}) collective-permute-start(bf16[2,128,1024]{2,1,0:T(8,128)(2,1)S(1)} %dynamic-slice_bitcast_fusion.6), channel_id=1, source_target_pairs={{0,8},{1,9},{2,10},{3,11},{4,12},{5,13},{6,14},{7,15},{8,0},{9,1},... | collective-permute-start | bytes 1572872 | tf_op jit(solution)/shard_map/ppermute | solution.py:156
  691.4 7.8 %collective-permute-start.23 = (bf16[2,32,3072]{2,1,0:T(8,128)(2,1)S(1)}, bf16[2,32,3072]{2,1,0:T(8,128)(2,1)S(1)}, u32[]{:S(2)}, u32[]{:S(2)}) collective-permute-start(bf16[2,32,3072]{2,1,0:T(8,128)(2,1)S(1)} %dynamic-slice_bitcast_fusion.9), channel_id=1, source_target_pairs={{0,1},{1,0},{2,3},{3,2},{4,5},{5,4},{6,7},{7,6},{8,9},{9,8},{10,11... | collective-permute-start | bytes 1179656 | tf_op jit(solution)/shard_map/ppermute | solution.py:156
  692.8 20.1 %collective-permute-start.34 = (bf16[32,4096]{1,0:T(8,128)(2,1)S(1)}, bf16[32,4096]{1,0:T(8,128)(2,1)S(1)}, u32[]{:S(2)}, u32[]{:S(2)}) collective-permute-start(bf16[32,4096]{1,0:T(8,128)(2,1)S(1)} %dynamic-slice_bitcast_fusion.11), channel_id=1, source_target_pairs={{0,16},{1,17},{2,18},{3,19},{4,20},{5,21},{6,22},{7,23},{8,24},{9,... | collective-permute-start | bytes 786440 | tf_op jit(solution)/shard_map/ppermute | solution.py:156
  694.2 24.4 %collective-permute-start.39 = (bf16[128,1024]{1,0:T(8,128)(2,1)S(1)}, bf16[128,1024]{1,0:T(8,128)(2,1)S(1)}, u32[]{:S(2)}, u32[]{:S(2)}) collective-permute-start(bf16[128,1024]{1,0:T(8,128)(2,1)S(1)} %dynamic-slice_bitcast_fusion.10), channel_id=1, source_target_pairs={{0,16},{1,17},{2,18},{3,19},{4,20},{5,21},{6,22},{7,23},{8,24},{9,... | collective-permute-start | bytes 786440 | tf_op jit(solution)/shard_map/ppermute | solution.py:156
  699.4 22.6 %collective-permute-start.24 = (bf16[32,3072]{1,0:T(8,128)(2,1)S(1)}, bf16[32,3072]{1,0:T(8,128)(2,1)S(1)}, u32[]{:S(2)}, u32[]{:S(2)}) collective-permute-start(bf16[32,3072]{1,0:T(8,128)(2,1)S(1)} %dynamic-slice_bitcast_fusion.13), channel_id=1, source_target_pairs={{0,16},{1,17},{2,18},{3,19},{4,20},{5,21},{6,22},{7,23},{8,24},{9,... | collective-permute-start | bytes 589832 | tf_op jit(solution)/shard_map/ppermute | solution.py:156
  (44 other events, 212.7 us)
Sparse Core Ops, SparseCore 0:
  10.9 73.8 all-gather.3
  88.3 99.8 all-gather.5
  191.3 77.8 all-gather.7
